TPU v7x, 256 devices: a whole 4x4x8 slice. The times are simulated.
256 devices in a mesh: sub: 16 (over x_hi, z), blk: 16 (over x_lo, y, core).
Axes of the slice: x: 4 (x_hi: 2, x_lo: 2; x = x_hi * 2 + x_lo), y: 4, z: 8, core: 2. Of those that a mesh axis runs over, the one named last changes fastest.
Arguments:
- coefficients: float32 [1024, 4, 2, 64, 128], P('sub', None, None, 'blk'), may hold values from -0.2 to 0.2
- owner_slot: int32 [1024], P('sub'), may hold values from 0 to 1023, as said below
- child_list: int32 [1024, 8], P('sub'), may hold values from 0 to 7, each once within a row
Outputs:
- children: float32 [1024, 4, 8, 64, 2, 128], P('sub', None, None, 'blk')
Inputs may be any that keep to these rules, and one draw needn't show every extreme that they name: owner_slot is a permutation of the 1024 positions; position s belongs to subtree index s // 64; of the 64 boxes held by one subtree index exactly 4 belong to each subtree index. `child_list`: each row lists the 8 octant codes once each.
All inputs are finite; a program needn't handle non-finite values.
Results may differ from a plain program's by a relative error of at most 0.0003.
Values sent between devices are 32-bit elements; how exact they have to be, the bound alone decides.
No kernel may reach another device: no remote copies, remote signals or barrier semaphores. Data moves between devices by JAX's collectives and lax.ppermute only.
A program may use at most 64 MiB of HBM per device.

v0:
```python
import jax
import jax.numpy as jnp
from jax import lax
from jax.sharding import PartitionSpec as P

L = 64
M = 128
J = 64
K = 128


def legendre_table(orders_abs, polar, degrees):
    cosines = jnp.cos(polar)[None, :]
    sines = jnp.sin(polar)[None, :]
    order_col = orders_abs[:, None]
    log_start = 0.5 * (
        jnp.log((2.0 * order_col + 1.0) / (4.0 * jnp.pi))
        + lax.lgamma(2.0 * order_col + 1.0)
        - order_col * jnp.log(4.0)
        - 2.0 * lax.lgamma(order_col + 1.0)
    ) + order_col * jnp.log(sines)
    diag_value = jnp.exp(log_start)
    next_value = jnp.sqrt(2.0 * order_col + 3.0) * cosines * diag_value

    def advance(state, degree):
        previous, before, factor_prev = state
        numer = jnp.maximum(4.0 * degree * degree - 1.0, 1.0)
        denom = jnp.maximum(degree * degree - order_col * order_col, 1.0)
        factor = jnp.sqrt(numer / denom)
        recur = factor * (cosines * previous - before / factor_prev)
        value = jnp.where(
            degree < order_col,
            0.0,
            jnp.where(
                degree == order_col,
                diag_value,
                jnp.where(degree == order_col + 1.0, next_value, recur),
            ),
        )
        return ((value, previous, factor), value)

    zeros = jnp.zeros_like(diag_value)
    start_state = (zeros, zeros, jnp.ones_like(order_col))
    _, values = lax.scan(advance, start_state, jnp.arange(degrees).astype(jnp.float32))
    return values


def dft_table(degrees, columns, azimuths):
    column_ids = jnp.arange(columns, dtype=jnp.int32)
    azimuth_ids = jnp.arange(azimuths, dtype=jnp.int32)
    turns = jnp.mod((column_ids[:, None] - degrees) * azimuth_ids[None, :], azimuths)
    angle = 2.0 * jnp.pi * turns.astype(jnp.float32) / azimuths
    cosine = jnp.cos(angle)
    sine = jnp.sin(angle)
    upper = jnp.concatenate([cosine, sine], axis=1)
    lower = jnp.concatenate([-sine, cosine], axis=1)
    return jnp.concatenate([upper, lower], axis=0)


def shift_children(waves, octants, polar, azimuths):
    azimuth = 2.0 * jnp.pi * jnp.arange(azimuths).astype(jnp.float32) / azimuths
    dir_x = jnp.sin(polar)[:, None] * jnp.cos(azimuth)[None, :]
    dir_y = jnp.sin(polar)[:, None] * jnp.sin(azimuth)[None, :]
    dir_z = jnp.cos(polar)[:, None] * jnp.ones_like(azimuth)[None, :]
    sign_x = (2 * (octants & 1) - 1).astype(jnp.float32)[:, None, None]
    sign_y = (2 * (octants >> 1 & 1) - 1).astype(jnp.float32)[:, None, None]
    sign_z = (2 * (octants >> 2 & 1) - 1).astype(jnp.float32)[:, None, None]
    phase = 5.5 * (sign_x * dir_x[None] + sign_y * dir_y[None] + sign_z * dir_z[None])
    phase_cos = jnp.cos(phase)[None]
    phase_sin = jnp.sin(phase)[None]
    wave_re = waves[:, :, 0, :][:, None]
    wave_im = waves[:, :, 1, :][:, None]
    real_part = wave_re * phase_cos - wave_im * phase_sin
    imag_part = wave_re * phase_sin + wave_im * phase_cos
    return jnp.stack([real_part, imag_part], axis=-2)


def body(coefficients, owner_slot, child_list):
    box_count = coefficients.shape[0]
    cases = coefficients.shape[1]
    sub_count = lax.axis_size("sub")
    per_peer = box_count // sub_count
    targets = owner_slot // box_count
    positions = owner_slot % box_count
    send_order = jnp.argsort(targets, stable=True)
    outgoing = coefficients[send_order].reshape((sub_count, per_peer) + coefficients.shape[1:])
    placed = positions[send_order].reshape(sub_count, per_peer)
    arrived, arrived_slots = (
        lax.all_to_all(outgoing, "sub", split_axis=0, concat_axis=0, tiled=True),
        lax.all_to_all(placed, "sub", split_axis=0, concat_axis=0, tiled=True),
    )
    restore = jnp.argsort(arrived_slots.reshape(-1))
    owned = arrived.reshape(coefficients.shape)[restore]
    blk_count = lax.axis_size("blk")
    blk_index = lax.axis_index("blk")
    cycle_width = J // blk_count
    polar_all = jnp.pi * (jnp.arange(J).astype(jnp.float32) + 0.5) / J
    polar_mine = lax.dynamic_slice_in_dim(polar_all, blk_index * cycle_width, cycle_width, 0)
    spectral = dft_table(L, M, K)
    width = M // blk_count
    column_start = blk_index * width
    orders_abs = jnp.abs(column_start + jnp.arange(width, dtype=jnp.int32) - L).astype(jnp.float32)
    table = legendre_table(orders_abs, polar_all, L)
    split_orders = lax.all_to_all(owned, "blk", split_axis=4, concat_axis=3, tiled=True)
    cycles = jnp.einsum("brxlc,lcj->brjxc", split_orders, table, precision=lax.Precision.HIGHEST)
    cycle_rows = lax.all_to_all(cycles, "blk", split_axis=2, concat_axis=4, tiled=True)
    waves = jnp.dot(
        cycle_rows.reshape(box_count * cases * cycle_width, 2 * M),
        spectral,
        precision=lax.Precision.HIGHEST,
    )
    waves = waves.reshape(box_count, cases, cycle_width, 2, K)
    return jax.vmap(shift_children, in_axes=(0, 0, None, None))(waves, child_list, polar_mine, K)


def solution(mesh):
    placed = (P("sub", None, None, "blk", None), P("sub"), P("sub", None))
    return jax.shard_map(
        body,
        mesh=mesh,
        in_specs=placed,
        out_specs=P("sub", None, None, "blk", None, None),
        check_vma=False,
    )
```

profile of v0, /device:TPU:1, one launch (start us, length us, event | category | flops | bytes accessed | tf_op | source)
XLA Modules:
  0.0 428.2 jit_solution(12758772600237134840)
XLA Ops:
  0.0 0.8 and_select_fusion
  0.8 2.0 sort.34
  2.8 0.8 gather_fusion.1
  3.6 0.7 all_to_all.34
  4.3 11.6 %all-to-all-start.1 = ((s32[16,1,4]{2,1,0:T(1,128)}), s32[16,1,4]{2,1,0:T(1,128)S(1)}, u32[]{:S(2)}, u32[]{:S(2)}) async-start(s32[16,1,4]{2,1,0:T(1,128)} %bitcast.3), calls=%async_computation.1 | async-start | bytes 16384 | tf_op jit(solution)/shard_map/all_to_all | solution.py:90
  15.9 2.1 gather_fusion
  17.9 6.6 %all-to-all-done.1 = s32[16,1,4]{2,1,0:T(1,128)S(1)} async-done(((s32[16,1,4]{2,1,0:T(1,128)}), s32[16,1,4]{2,1,0:T(1,128)S(1)}, u32[]{:S(2)}, u32[]{:S(2)}) %all-to-all-start.1) | async-done | bytes 288 | tf_op jit(solution)/shard_map/all_to_all | solution.py:90
  24.5 3.7 all-to-all-start
  28.9 0.6 reduce.3
  29.7 2.1 sort.35
  31.7 21.8 %all-to-all-done = f32[16,4,4,2,4,128]{5,4,3,2,1,0:T(4,128)S(1)} async-done(((f32[16,4,4,2,4,128]{5,4,3,2,1,0:T(4,128)}), f32[16,4,4,2,4,128]{5,4,3,2,1,0:T(4,128)S(1)}, u32[]{:S(2)}, u32[]{:S(2)}) %all-to-all-start) | async-done | bytes 1048608 | tf_op jit(solution)/shard_map/all_to_all | solution.py:89
  53.6 2.1 gather_fusion.2
  55.7 2.7 copy.47
  58.3 2.9 reshape.516
  61.2 8.7 %all-to-all-start.2 = ((f32[16,1,16384]{2,1,0:T(1,128)}), f32[16,1,16384]{2,1,0:T(1,128)S(1)}, u32[]{:S(2)}, u32[]{:S(2)}) async-start(f32[16,1,16384]{2,1,0:T(1,128)} %reshape.516), calls=%async_computation.2 | async-start | bytes 2097152 | tf_op jit(solution)/shard_map/all_to_all | solution.py:104
  70.0 289.6 %while.21 = (s32[]{:T(128)}, f32[8,64]{1,0:T(8,128)S(1)}, f32[8,64]{1,0:T(8,128)S(1)}, f32[8,1]{0,1:T(1,128)S(1)}, f32[64,8,64]{2,1,0:T(8,128)S(1)}, /*index=5*/...) while((s32[]{:T(128)}, f32[8,64]{1,0:T(8,128)S(1)}, ...), condition=%wide.region_1.2_spmd.clone.clone.clone, body=%wide.region_0.1_spmd.clone.clone.clone.sunk | while | flops 6576 | bytes 26812 | solution.py:44
  154.5 0.6 compare_bitcast_fusion.6
  240.4 0.6 compare_bitcast_fusion.6
  360.2 4.4 %reduce.4 = f32[16,16384]{1,0:T(8,128)} reduce(f32[16,1,16384]{2,1,0:T(1,128)S(1)} %all-to-all-done.2, f32[]{:T(128)} %broadcast.950), dimensions={1}, to_apply=%all_to_all.36.reduce_sub_computation | reduce | bytes 2097156 | tf_op jit(solution)/shard_map/all_to_all | solution.py:104
  364.6 2.6 reshape.517
  367.2 1.2 copy.75
  368.7 2.2 fusion.20
  370.9 1.6 copy.76
  372.6 3.2 reshape.518
  375.8 5.7 %all-to-all-start.3 = ((f32[16,1,16384]{2,1,0:T(1,128)}), f32[16,1,16384]{2,1,0:T(1,128)S(1)}, u32[]{:S(2)}, u32[]{:S(2)}) async-start(f32[16,1,16384]{2,1,0:T(1,128)} %reshape.518), calls=%async_computation.3 | async-start | bytes 2097152 | tf_op jit(solution)/shard_map/all_to_all | solution.py:106
  382.3 9.2 %fusion.24 = (f32[64,8,4,128]{3,2,1,0:T(4,128)}, f32[64,8,4,128]{3,2,1,0:T(4,128)}) fusion(f32[4]{0:T(128)S(1)} %get-tuple-element.329, f32[64,8]{1,0:T(8,128)S(1)} %copy.58, f32[4,128]{1,0:T(4,128)S(1)} %get-tuple-element.327, f32[64,8]{1,0:T(8,128)S(1)} %copy.57, f32[4,128]{1,0:T(4,128)S(1)} %get-tuple-element.326, f32[64,8]{1,0:T(8,128)S(1)} %copy.56), kind=kLoop, calls=%fused_computation.36 | loop fusion | flops 1572864 | bytes 2107408 | tf_op jit(solution)/shard_map/vmap()/cos | solution.py:69
  391.4 5.9 %all-to-all-done.3 = f32[16,1,16384]{2,1,0:T(1,128)S(1)} async-done(((f32[16,1,16384]{2,1,0:T(1,128)}), f32[16,1,16384]{2,1,0:T(1,128)S(1)}, u32[]{:S(2)}, u32[]{:S(2)}) %all-to-all-start.3) | async-done | bytes 1048608 | tf_op jit(solution)/shard_map/all_to_all | solution.py:106
  397.3 4.4 %reduce.5 = f32[16,16384]{1,0:T(8,128)} reduce(f32[16,1,16384]{2,1,0:T(1,128)S(1)} %all-to-all-done.3, f32[]{:T(128)} %broadcast.950), dimensions={1}, to_apply=%all_to_all.40.reduce_sub_computation | reduce | bytes 2097156 | tf_op jit(solution)/shard_map/all_to_all | solution.py:106
  401.8 2.7 reshape.519
  404.9 3.5 fusion.47
  409.2 9.8 %multiply_subtract_fusion.1 = (f32[64,4,8,4,1,128]{5,4,3,2,1,0:T(1,128)S(1)}, f32[64,4,8,4,1,128]{5,4,3,2,1,0:T(1,128)S(1)}) fusion(f32[64,8,4,128]{3,2,1,0:T(4,128)S(1)} %copy-done.2, f32[64,4,4,128]{3,2,1,0:T(4,128)S(1)} %copy.59, f32[64,8,4,128]{3,2,1,0:T(4,128)S(1)} %copy-done.1, f32[64,4,4,128]{3,2,1,0:T(4,128)S(1)} %copy.55), kind=kLoop, calls=%fused_computation.29 | loop fusion | flops 6291456 | bytes 11534336 | tf_op jit(solution)/shard_map/vmap()/sub | solution.py:73
  419.1 9.2 %pad_maximum_fusion = f32[64,4,8,4,2,128]{5,4,3,2,1,0:T(2,128)} fusion(f32[64,4,8,4,1,128]{5,4,3,2,1,0:T(1,128)S(1)} %get-tuple-element.313, f32[64,4,8,4,1,128]{5,4,3,2,1,0:T(1,128)S(1)} %get-tuple-element.312), kind=kLoop, calls=%fused_computation.27 | loop fusion | flops 2097152 | bytes 16777216 | tf_op jit(solution)/shard_map/vmap()/stack | solution.py:75
  (552 shorter events, 133.0 us)
Async XLA Ops:
  0.0 15.9 %copy-start = (f32[64,4,2,4,128]{4,3,2,1,0:T(4,128)S(1)}, f32[64,4,2,4,128]{4,3,2,1,0:T(4,128)}, u32[]{:S(2)}) copy-start(f32[64,4,2,4,128]{4,3,2,1,0:T(4,128)} %param.5) | copy-start | bytes 3145732
  4.3 20.2 %all-to-all-start.1 = ((s32[16,1,4]{2,1,0:T(1,128)}), s32[16,1,4]{2,1,0:T(1,128)S(1)}, u32[]{:S(2)}, u32[]{:S(2)}) async-start(s32[16,1,4]{2,1,0:T(1,128)} %bitcast.3), calls=%async_computation.1 | async-start | bytes 16384 | tf_op jit(solution)/shard_map/all_to_all | solution.py:90
  24.5 29.1 %all-to-all-start = ((f32[16,4,4,2,4,128]{5,4,3,2,1,0:T(4,128)}), f32[16,4,4,2,4,128]{5,4,3,2,1,0:T(4,128)S(1)}, u32[]{:S(2)}, u32[]{:S(2)}) async-start(f32[16,4,4,2,4,128]{5,4,3,2,1,0:T(4,128)} %bitcast.1), calls=%async_computation | async-start | bytes 2097152 | tf_op jit(solution)/shard_map/all_to_all | solution.py:89
  55.6 304.0 %copy-start.3 = (s32[64,8]{0,1:T(8,128)S(1)}, s32[64,8]{0,1:T(8,128)}, u32[]{:S(2)}) copy-start(s32[64,8]{0,1:T(8,128)} %param.7) | copy-start | bytes 6148
  61.2 298.4 %all-to-all-start.2 = ((f32[16,1,16384]{2,1,0:T(1,128)}), f32[16,1,16384]{2,1,0:T(1,128)S(1)}, u32[]{:S(2)}, u32[]{:S(2)}) async-start(f32[16,1,16384]{2,1,0:T(1,128)} %reshape.516), calls=%async_computation.2 | async-start | bytes 2097152 | tf_op jit(solution)/shard_map/all_to_all | solution.py:104
  375.8 21.6 %all-to-all-start.3 = ((f32[16,1,16384]{2,1,0:T(1,128)}), f32[16,1,16384]{2,1,0:T(1,128)S(1)}, u32[]{:S(2)}, u32[]{:S(2)}) async-start(f32[16,1,16384]{2,1,0:T(1,128)} %reshape.518), calls=%async_computation.3 | async-start | bytes 2097152 | tf_op jit(solution)/shard_map/all_to_all | solution.py:106
  404.9 4.3 %copy-start.1 = (f32[64,8,4,128]{3,2,1,0:T(4,128)S(1)}, f32[64,8,4,128]{3,2,1,0:T(4,128)}, u32[]{:S(2)}) copy-start(f32[64,8,4,128]{3,2,1,0:T(4,128)} %get-tuple-element.316) | copy-start | bytes 3145732
  404.9 4.3 %copy-start.2 = (f32[64,8,4,128]{3,2,1,0:T(4,128)S(1)}, f32[64,8,4,128]{3,2,1,0:T(4,128)}, u32[]{:S(2)}) copy-start(f32[64,8,4,128]{3,2,1,0:T(4,128)} %get-tuple-element.317) | copy-start | bytes 3145732
where the time goes:
time: 432 us; the launch traced here: 428 us
  loops' own time  159 us (37%)
  other arithmetic  134 us (31%)
  local copies, waits for them, and re-layouts  65.2 us (15%)
  waiting for transfers between devices  34.3 us (8%)
  starting transfers between devices  29.7 us (7%)
  matrix products  5.7 us (1%)
    another operation x1, loops' own time, legendre_table(): lax.scan(advance, start_state, jnp.arange(degrees).astype(jnp.float32))  159 us
    lt x64, other arithmetic, advance(): degree < order_col  40.2 us
    eq x64, other arithmetic, advance(): degree == order_col + 1.0  39.8 us
    dynamic_slice x64, local copies, waits for them, and re-layouts, legendre_table(): lax.scan(advance, start_state, jnp.arange(degrees).astype(jnp.float32))  39.6 us
    all_to_all x1, waiting for transfers between devices, body(): lax.all_to_all(outgoing, 'sub', split_axis=0, concat_axis=0, tiled=True)  21.8 us
    all_to_all x1, starting transfers between devices, body(): lax.all_to_all(placed, 'sub', split_axis=0, concat_axis=0, tiled=True)  11.6 us
    unnamed x12, local copies, waits for them, and re-layouts  11.5 us
    sub x1, other arithmetic, shift_children(): real_part = wave_re * phase_cos - wave_im * phase_sin  9.82 us
  transfers between devices with their start and end apart: 4, of which 3 were waited for; matrix products, arithmetic and copies ran while one was open for 34% of the time, Pallas kernels for 0%

commit v1 on v0

v1 whole, which is shorter than its diff:
```python
import math

import jax
import jax.numpy as jnp
import ml_dtypes
import numpy as np
from jax import lax
from jax.experimental import pallas as pl
from jax.experimental.pallas import tpu as pltpu
from jax.sharding import PartitionSpec as P

L = 64
M = 128
J = 64
K = 128
HALF = J // 2
F32 = jnp.float32
BF16 = jnp.bfloat16


def legendre_half():
    order = np.abs(np.arange(M) - L).astype(np.float64)[None, :]
    polar = (np.pi * (np.arange(HALF) + 0.5) / J)[:, None]
    cosines, sines = np.cos(polar), np.sin(polar)
    lgamma = np.vectorize(math.lgamma)
    start = np.exp(
        0.5 * (np.log((2 * order + 1) / (4 * np.pi)) + lgamma(2 * order + 1) - order * np.log(4.0) - 2 * lgamma(order + 1))
        + order * np.log(sines)
    )
    following = np.sqrt(2 * order + 3) * cosines * start
    previous = before = np.zeros_like(start)
    factor_before = np.ones_like(order)
    rows = []
    for degree in range(L):
        factor = np.sqrt(np.maximum(4.0 * degree * degree - 1, 1) / np.maximum(degree * degree - order * order, 1))
        recur = factor * (cosines * previous - before / factor_before)
        value = np.where(degree < order, 0.0, np.where(degree == order, start, np.where(degree == order + 1, following, recur)))
        rows.append(value)
        previous, before, factor_before = value, previous, factor
    return np.stack(rows).astype(np.float32)


def dft_halves():
    turns = ((np.arange(M)[:, None] - L) * np.arange(K)[None, :]) % K
    angle = 2 * np.pi * turns / K
    cosine, sine = np.cos(angle), np.sin(angle)
    full = np.block([[cosine, sine], [-sine, cosine]])
    high = full.astype(ml_dtypes.bfloat16)
    rest = (full - high.astype(np.float64)).astype(ml_dtypes.bfloat16)
    return high, rest


def shift_tables(blk_count):
    polar = np.pi * (np.arange(J) + 0.5) / J
    azimuth = 2 * np.pi * np.arange(K) / K
    octant = np.arange(8)
    sign = [(2 * ((octant >> bit) & 1) - 1)[:, None, None] for bit in range(3)]
    phase = 5.5 * (
        sign[0] * (np.sin(polar)[:, None] * np.cos(azimuth))[None]
        + sign[1] * (np.sin(polar)[:, None] * np.sin(azimuth))[None]
        + sign[2] * (np.cos(polar)[:, None] * np.ones(K))[None]
    )
    cosine = np.stack([np.cos(phase), np.cos(phase)], axis=2)
    sine = np.stack([-np.sin(phase), np.sin(phase)], axis=2)
    width = J // blk_count

    def cut(table):
        table = table.reshape(8, blk_count, width * 2, K)
        return np.ascontiguousarray(table.transpose(1, 0, 2, 3)).astype(np.float32)

    return cut(cosine), cut(sine)


def pack_kernel(sub_count, me_ref, slot_ref, coef_ref, out_ref, place_ref, count):
    box_count = coef_ref.shape[0]
    per_peer = box_count // sub_count
    for peer in range(sub_count):
        count[peer] = 0
    row = lax.broadcasted_iota(jnp.int32, place_ref.shape, 0)
    lane = lax.broadcasted_iota(jnp.int32, place_ref.shape, 1)
    first = me_ref[0] * per_peer
    place = jnp.zeros(place_ref.shape, jnp.int32)
    for box in range(box_count):
        slot = slot_ref[box]
        peer = slot // box_count
        rank = count[peer]
        count[peer] = rank + 1
        out_ref[peer * per_peer + rank] = coef_ref[box]
        here = (row == peer) & (lane == first + rank)
        place = jnp.where(here, slot - peer * box_count, place)
    place_ref[...] = place


def spread(value, order):
    return jnp.take_along_axis(value, order, axis=0)


def transform_kernel(blk_count, in_ref, table_ref, high_ref, rest_ref, out_ref, cycles):
    boxes = in_ref.shape[0] // blk_count
    degrees = L // blk_count
    group = 2
    vregs = HALF // 8
    lane = lax.broadcasted_iota(jnp.int32, (8, M), 1)
    mirror = jnp.where(lane % 2 == 0, 1.0, -1.0).astype(F32)

    def legendre(step, carry):
        sums = [[[None] * vregs for _ in range(2)] for _ in range(2 * group)]
        for degree in range(L):
            source, row = degree // degrees, degree % degrees
            table = [table_ref[degree, 8 * v : 8 * v + 8, :] for v in range(vregs)]
            for one in range(2 * group):
                box, part = step * group + one // 2, one % 2
                at = part * degrees + row
                value = in_ref[box * blk_count + source, at : at + 1, :]
                wide = jnp.broadcast_to(value, (8, M))
                for v in range(vregs):
                    term = wide * table[v]
                    old = sums[one][degree % 2][v]
                    sums[one][degree % 2][v] = term if old is None else old + term
        for one in range(2 * group):
            box, part = step * group + one // 2, one % 2
            for v in range(vregs):
                even, odd = sums[one][0][v], sums[one][1][v]
                low = pl.multiple_of(box * J + 8 * v, 8)
                high = pl.multiple_of(box * J + HALF + 8 * v, 8)
                cycles[pl.ds(low, 8), part * M : part * M + M] = even + odd
                cycles[pl.ds(high, 8), part * M : part * M + M] = (even - odd) * mirror
        return carry

    lax.fori_loop(0, boxes // group, legendre, 0)

    width = J // blk_count
    sub_row = lax.broadcasted_iota(jnp.int32, (8, K), 0)
    real_row = sub_row % 2 == 0
    step_row = sub_row // 2
    chunk = 4

    def azimuths(step, carry):
        base = pl.multiple_of(step * (chunk * J), chunk * J)
        left = cycles[pl.ds(base, chunk * J), :]
        left_high = left.astype(BF16)
        left_rest = (left - left_high.astype(F32)).astype(BF16)
        waves = jnp.dot(left_high, high_ref[...], preferred_element_type=F32)
        waves += jnp.dot(left_rest, high_ref[...], preferred_element_type=F32)
        waves += jnp.dot(left_high, rest_ref[...], preferred_element_type=F32)
        for one in range(chunk):
            for blk in range(blk_count):
                first = blk * width
                if first < HALF:
                    at, order = first // 8 * 8, first % 8 + step_row
                else:
                    low = J - 1 - first
                    at, order = HALF + low // 8 * 8, low % 8 - step_row
                start = one * J + at
                real = spread(waves[start : start + 8, :K], order)
                imag = spread(waves[start : start + 8, K:], order)
                out_ref[blk, step * chunk + one] = jnp.where(real_row, real, imag)
        return carry

    lax.fori_loop(0, boxes // chunk, azimuths, 0)


def shift_kernel(boxes, sub_count, me_ref, place_ref, child_ref, in_ref, cos_ref, sin_ref, out_ref, inverse):
    per_peer = boxes // sub_count
    cases = 4

    @pl.when(pl.program_id(0) == 0)
    def _():
        for arrival in range(boxes):
            inverse[place_ref[arrival]] = arrival

    even = lax.broadcasted_iota(jnp.int32, (8, K), 0) % 2 == 0
    count = out_ref.shape[0]

    def one_box(at, carry):
        box = pl.program_id(0) * count + at
        arrival = inverse[box]
        source = arrival // per_peer
        rank = arrival % per_peer
        waves = [in_ref[rank * cases + case, source] for case in range(cases)]
        crossed = [jnp.where(even, pltpu.roll(w, 7, 0), pltpu.roll(w, 1, 0)) for w in waves]
        for child in range(8):
            octant = child_ref[box, child]
            cosine, sine = cos_ref[0, octant], sin_ref[0, octant]
            for case in range(cases):
                out_ref[at, case * 8 + child] = waves[case] * cosine + crossed[case] * sine
        return carry

    lax.fori_loop(0, count, one_box, 0)


def body(coefficients, owner_slot, child_list):
    box_count, cases = coefficients.shape[:2]
    sub_count = lax.axis_size("sub")
    blk_count = lax.axis_size("blk")
    per_peer = box_count // sub_count
    vmem = pl.BlockSpec(memory_space=pltpu.VMEM)
    smem = pl.BlockSpec(memory_space=pltpu.SMEM)
    sub_index = lax.axis_index("sub").reshape(1)
    blk_index = lax.axis_index("blk").reshape(1)

    outgoing, places = pl.pallas_call(
        lambda *refs: pack_kernel(sub_count, *refs),
        out_shape=(
            jax.ShapeDtypeStruct((box_count, cases * 8, M), F32),
            jax.ShapeDtypeStruct((sub_count, box_count), jnp.int32),
        ),
        in_specs=[smem, smem, vmem],
        out_specs=(vmem, vmem),
        scratch_shapes=[pltpu.SMEM((sub_count,), jnp.int32)],
        name="pack",
    )(sub_index, owner_slot, coefficients.reshape(box_count, cases * 8, M))
    arrived_places = lax.psum_scatter(places, "sub", scatter_dimension=0, tiled=False)

    arrived = lax.all_to_all(outgoing.reshape(box_count * cases, 8, M), ("sub", "blk"), 0, 0, tiled=True)

    high, rest = dft_halves()
    waves = pl.pallas_call(
        lambda *refs: transform_kernel(blk_count, *refs),
        out_shape=jax.ShapeDtypeStruct((blk_count, sub_count, 8, K), F32),
        in_specs=[vmem] * 4,
        out_specs=vmem,
        scratch_shapes=[pltpu.VMEM((sub_count * J, 2 * M), F32)],
        name="transform",
    )(arrived, jnp.asarray(legendre_half()), jnp.asarray(high), jnp.asarray(rest))

    rows = lax.all_to_all(waves, "blk", 0, 0, tiled=True)

    cosine, sine = shift_tables(blk_count)
    step = 4
    children = pl.pallas_call(
        lambda *refs: shift_kernel(box_count, sub_count, *refs),
        out_shape=jax.ShapeDtypeStruct((box_count, cases * 8, 8, K), F32),
        grid_spec=pltpu.PrefetchScalarGridSpec(
            num_scalar_prefetch=3,
            grid=(box_count // step,),
            in_specs=[
                vmem,
                pl.BlockSpec((1, 8, 8, K), lambda i, me, place, child: (me[0], 0, 0, 0)),
                pl.BlockSpec((1, 8, 8, K), lambda i, me, place, child: (me[0], 0, 0, 0)),
            ],
            out_specs=pl.BlockSpec((step, cases * 8, 8, K), lambda i, me, place, child: (i, 0, 0, 0)),
            scratch_shapes=[pltpu.SMEM((box_count,), jnp.int32)],
        ),
        name="shift",
    )(blk_index, arrived_places, child_list, rows, jnp.asarray(cosine), jnp.asarray(sine))
    return children.reshape(box_count, cases, 8, J // blk_count, 2, K)


def solution(mesh):
    placed = (P("sub", None, None, "blk", None), P("sub"), P("sub", None))
    return jax.shard_map(
        body,
        mesh=mesh,
        in_specs=placed,
        out_specs=P("sub", None, None, "blk", None, None),
        check_vma=False,
    )
```

time: 432 us -> 87 us (0.20)
  loops' own time: 159 us -> 0 us
  other arithmetic: 134 us -> 0 us
  local copies, waits for them, and re-layouts: 65.2 us -> 3.46 us
  blocking collectives: 0 us -> 58.5 us
  waiting for transfers between devices: 34.3 us -> 0.87 us
  starting transfers between devices: 29.7 us -> 4.93 us
  Pallas kernels: 0 us -> 18.5 us
  matrix products: 5.7 us -> 0 us
    another operation x1 -> x0, loops' own time: 159 us -> none  [legendre_table(): lax.scan(advance, start_state, jnp.arange(degrees).astype(jnp.float32))]
    all_to_all x0 -> x1, blocking collectives: none -> 46 us  [body(): lax.all_to_all(outgoing.reshape(box_count * cases, 8, M), ('sub', 'blk'),...]
    lt x64 -> x0, other arithmetic: 40.2 us -> none  [advance(): degree < order_col]
    eq x64 -> x0, other arithmetic: 39.8 us -> none  [advance(): degree == order_col + 1.0]
    dynamic_slice x64 -> x0, local copies, waits for them, and re-layouts: 39.6 us -> none  [legendre_table(): lax.scan(advance, start_state, jnp.arange(degrees).astype(jnp.float32))]
    all_to_all x4 -> x1, waiting for transfers between devices: 34.3 us -> 0.87 us  [body(): rows = lax.all_to_all(waves, 'blk', 0, 0, tiled=True)]
    all_to_all x4 -> x1, starting transfers between devices: 29.7 us -> 4.93 us  [body(): rows = lax.all_to_all(waves, 'blk', 0, 0, tiled=True)]
    pallas_call x0 -> x3, Pallas kernels: none -> 18.5 us  [the longest x1 9.85 us: body(): pl.pallas_call(lambda *refs: shift_kernel(box_count, sub_count, *refs), o...]
  transfers between devices with their start and end apart: 4 -> 1, of which waited for: 3 -> 1; matrix products, arithmetic and copies ran while one was open for 34% -> 3% of each run, Pallas kernels for 0% -> 0%
where the time goes in v1:
time: 87 us; the launch traced here: 86.3 us
  blocking collectives  58.5 us (67%)
  Pallas kernels  18.5 us (21%)
  starting transfers between devices  4.93 us (6%)
  local copies, waits for them, and re-layouts  3.46 us (4%)
  waiting for transfers between devices  0.87 us (1%)
    all_to_all x1, blocking collectives, body(): lax.all_to_all(outgoing.reshape(box_count * cases, 8, M), ('sub', 'blk'),...  46 us
    unnamed x1, blocking collectives  12.5 us
    pallas_call x1, Pallas kernels, body(): pl.pallas_call(lambda *refs: shift_kernel(box_count, sub_count, *refs), o...  9.85 us
    pallas_call x1, Pallas kernels, body(): pl.pallas_call(lambda *refs: transform_kernel(blk_count, *refs), out_shap...  5.9 us
    all_to_all x1, starting transfers between devices, body(): rows = lax.all_to_all(waves, 'blk', 0, 0, tiled=True)  4.93 us
    pallas_call x1, Pallas kernels, body(): pl.pallas_call(lambda *refs: pack_kernel(sub_count, *refs), out_shape=(ja...  2.78 us
    unnamed x8, local copies, waits for them, and re-layouts  2.28 us
  transfers between devices with their start and end apart: 1, of which 1 were waited for; matrix products, arithmetic and copies ran while one was open for 3% of the time, Pallas kernels for 0%

profile of v1, /device:TPU:1, one launch (start us, length us, event | category | flops | bytes accessed | tf_op | source)
XLA Modules:
  0.0 86.3 jit_solution(22175512607474961)
XLA Ops:
  0.0 0.0 copy-start.2
  0.0 0.0 copy-start.1
  0.0 2.8 %pack.1 = (f32[64,32,128]{2,1,0:T(8,128)}, s32[16,64]{1,0:T(8,128)}) custom-call(s32[1]{0:T(128)} %bitcast.1.refs_0_, s32[64]{0:T(128)} %refs_1_.2, f32[64,32,128]{2,1,0:T(8,128)} %bitcast.8), custom_call_target="tpu_custom_call" | custom-call | tf_op jit(solution)/shard_map/pack/pallas_call | solution.py:202
  2.8 46.0 %all_to_all.10.refs_0_ = f32[256,8,128]{2,1,0:T(8,128)} all-to-all(f32[256,8,128]{2,1,0:T(8,128)} %bitcast.9), channel_id=1, replica_groups=mesh['sub'=16,'blk'=16] {'sub','blk'}, dimensions={0} | all-to-all | bytes 2097152 | tf_op jit(solution)/shard_map/all_to_all | solution.py:215
  48.8 5.9 %transform.1 = f32[16,16,8,128]{3,2,1,0:T(8,128)} custom-call(f32[256,8,128]{2,1,0:T(8,128)} %all_to_all.10.refs_0_, f32[64,32,128]{2,1,0:T(8,128)} %constant.17.clone.refs_1_, bf16[256,256]{1,0:T(8,128)(2,1)} %constant.18.clone.refs_2_, bf16[256,256]{1,0:T(8,128)(2,1)} %constant.19.clone.refs_3_), custom_call_target="tpu_custom_call" | custom-call | tf_op jit(solution)/shard_map/transform/pallas_call | solution.py:218
  54.7 4.9 %all-to-all-start.1 = ((f32[16,16,8,128]{3,2,1,0:T(8,128)}), f32[16,16,8,128]{3,2,1,0:T(8,128)S(1)}, u32[]{:S(2)}, u32[]{:S(2)}) async-start(f32[16,16,8,128]{3,2,1,0:T(8,128)} %transform.1), calls=%async_computation.1 | async-start | bytes 2097152 | tf_op jit(solution)/shard_map/all_to_all | solution.py:227
  59.6 0.0 copy-done.1
  59.6 0.7 copy.10.refs_2_
  60.3 0.0 copy-done.2
  60.3 0.6 dynamic-slice
  60.9 12.5 %all-reduce = s32[16,64]{1,0:T(8,128)S(1)} all-reduce(s32[16,64]{1,0:T(8,128)} %get-tuple-element.7), channel_id=2, replica_groups=mesh['sub'=16,'blk'=16] {'sub'}, use_global_device_ids=true, to_apply=%region_0.0.clone | all-reduce | flops 1024 | bytes 8192
  73.4 1.2 %dynamic-slice_bitcast_fusion.refs_1_ = s32[64]{0:T(128)} fusion(s32[16,64]{1,0:T(8,128)S(1)} %all-reduce, u32[]{:T(128)} %bitcast.3), kind=kLoop, calls=%fused_computation | loop fusion | bytes 516 | tf_op jit(solution)/shard_map/reduce_scatter | solution.py:213
  74.6 0.9 %all-to-all-done.1.refs_3_ = f32[16,16,8,128]{3,2,1,0:T(8,128)S(1)} async-done(((f32[16,16,8,128]{3,2,1,0:T(8,128)}), f32[16,16,8,128]{3,2,1,0:T(8,128)S(1)}, u32[]{:S(2)}, u32[]{:S(2)}) %all-to-all-start.1) | async-done | bytes 1048608 | tf_op jit(solution)/shard_map/all_to_all | solution.py:227
  75.5 0.0 copy-start
  75.5 1.0 %copy-done = f32[16,16,8,128]{3,2,1,0:T(8,128)} copy-done((f32[16,16,8,128]{3,2,1,0:T(8,128)}, f32[16,16,8,128]{3,2,1,0:T(8,128)S(1)}, u32[]{:S(2)}) %copy-start) | copy-done | bytes 1048600
  76.5 9.9 %shift.1 = f32[64,32,8,128]{3,2,1,0:T(8,128)} custom-call(s32[1]{0:T(128)} %bitcast.refs_0_, s32[64]{0:T(128)} %dynamic-slice_bitcast_fusion.refs_1_, s32[64,8]{1,0:T(8,128)} %copy.10.refs_2_, f32[16,16,8,128]{3,2,1,0:T(8,128)} %copy-done, f32[16,8,8,128]{3,2,1,0:T(8,128)} %constant.20.clone.refs_4_, f32[16,8,8,128]{3,2,1,0:T(8,128)} %constant.21.clone.refs_5_), custom_call_target="tpu_custom_call" | custom-call | tf_op jit(solution)/shard_map/shift/pallas_call | solution.py:231
Async XLA Ops:
  0.0 60.3 %copy-start.2 = (u32[256]{0:T(256)S(1)}, u32[256]{0:T(256)}, u32[]{:S(2)}) copy-start(u32[256]{0:T(256)} %constant.25) | copy-start | bytes 3076
  0.0 59.6 %copy-start.1 = (s32[64,8]{0,1:T(8,128)S(1)}, s32[64,8]{0,1:T(8,128)}, u32[]{:S(2)}) copy-start(s32[64,8]{0,1:T(8,128)} %param.10) | copy-start | bytes 6148
  54.7 20.8 %all-to-all-start.1 = ((f32[16,16,8,128]{3,2,1,0:T(8,128)}), f32[16,16,8,128]{3,2,1,0:T(8,128)S(1)}, u32[]{:S(2)}, u32[]{:S(2)}) async-start(f32[16,16,8,128]{3,2,1,0:T(8,128)} %transform.1), calls=%async_computation.1 | async-start | bytes 2097152 | tf_op jit(solution)/shard_map/all_to_all | solution.py:227
  75.5 1.0 %copy-start = (f32[16,16,8,128]{3,2,1,0:T(8,128)}, f32[16,16,8,128]{3,2,1,0:T(8,128)S(1)}, u32[]{:S(2)}) copy-start(f32[16,16,8,128]{3,2,1,0:T(8,128)S(1)} %all-to-all-done.1.refs_3_) | copy-start | bytes 3145732

commit v2 on v1

--- a/solution.py
+++ b/solution.py
@@ -71,7 +71,7 @@
     return cut(cosine), cut(sine)
 
 
-def pack_kernel(sub_count, me_ref, slot_ref, coef_ref, out_ref, place_ref, count):
+def pack_kernel(sub_count, me_ref, slot_ref, coef_ref, out_ref, place_ref, count, moved):
     box_count = coef_ref.shape[0]
     per_peer = box_count // sub_count
     for peer in range(sub_count):
@@ -85,17 +85,34 @@
         peer = slot // box_count
         rank = count[peer]
         count[peer] = rank + 1
-        out_ref[peer * per_peer + rank] = coef_ref[box]
+        pltpu.make_async_copy(coef_ref.at[box], out_ref.at[peer * per_peer + rank], moved).start()
         here = (row == peer) & (lane == first + rank)
         place = jnp.where(here, slot - peer * box_count, place)
     place_ref[...] = place
+    pltpu.make_async_copy(coef_ref, out_ref, moved).wait()
 
 
 def spread(value, order):
     return jnp.take_along_axis(value, order, axis=0)
 
 
-def transform_kernel(blk_count, in_ref, table_ref, high_ref, rest_ref, out_ref, cycles):
+def transform_kernel(
+    blk_count, in_ref, table_hbm, high_hbm, rest_hbm, place_ref, out_ref,
+    table_ref, high_ref, rest_ref, cycles, made, table_in, dft_in, moved,
+):
+    del place_ref
+    pieces = table_in.shape[0]
+    cut = L // pieces
+    arriving = []
+    for piece in range(pieces):
+        part = pl.ds(piece * cut, cut)
+        arriving.append(pltpu.make_async_copy(table_hbm.at[part], table_ref.at[part], table_in.at[piece]))
+    dft = [
+        pltpu.make_async_copy(high_hbm, high_ref, dft_in.at[0]),
+        pltpu.make_async_copy(rest_hbm, rest_ref, dft_in.at[1]),
+    ]
+    for copy in arriving + dft:
+        copy.start()
     boxes = in_ref.shape[0] // blk_count
     degrees = L // blk_count
     group = 2
@@ -103,10 +120,12 @@
     lane = lax.broadcasted_iota(jnp.int32, (8, M), 1)
     mirror = jnp.where(lane % 2 == 0, 1.0, -1.0).astype(F32)
 
-    def legendre(step, carry):
+    def legendre(step, slot, first=False):
         sums = [[[None] * vregs for _ in range(2)] for _ in range(2 * group)]
         for degree in range(L):
             source, row = degree // degrees, degree % degrees
+            if first and degree % cut == 0:
+                arriving[degree // cut].wait()
             table = [table_ref[degree, 8 * v : 8 * v + 8, :] for v in range(vregs)]
             for one in range(2 * group):
                 box, part = step * group + one // 2, one % 2
@@ -118,32 +137,26 @@
                     old = sums[one][degree % 2][v]
                     sums[one][degree % 2][v] = term if old is None else old + term
         for one in range(2 * group):
-            box, part = step * group + one // 2, one % 2
+            box, part = one // 2, one % 2
             for v in range(vregs):
                 even, odd = sums[one][0][v], sums[one][1][v]
-                low = pl.multiple_of(box * J + 8 * v, 8)
-                high = pl.multiple_of(box * J + HALF + 8 * v, 8)
-                cycles[pl.ds(low, 8), part * M : part * M + M] = even + odd
-                cycles[pl.ds(high, 8), part * M : part * M + M] = (even - odd) * mirror
-        return carry
-
-    lax.fori_loop(0, boxes // group, legendre, 0)
+                low, high = box * J + 8 * v, box * J + HALF + 8 * v
+                cycles[slot, low : low + 8, part * M : part * M + M] = even + odd
+                cycles[slot, high : high + 8, part * M : part * M + M] = (even - odd) * mirror
 
     width = J // blk_count
     sub_row = lax.broadcasted_iota(jnp.int32, (8, K), 0)
     real_row = sub_row % 2 == 0
     step_row = sub_row // 2
-    chunk = 4
-
-    def azimuths(step, carry):
-        base = pl.multiple_of(step * (chunk * J), chunk * J)
-        left = cycles[pl.ds(base, chunk * J), :]
+
+    def azimuths(step, slot):
+        left = cycles[slot]
         left_high = left.astype(BF16)
         left_rest = (left - left_high.astype(F32)).astype(BF16)
         waves = jnp.dot(left_high, high_ref[...], preferred_element_type=F32)
         waves += jnp.dot(left_rest, high_ref[...], preferred_element_type=F32)
         waves += jnp.dot(left_high, rest_ref[...], preferred_element_type=F32)
-        for one in range(chunk):
+        for one in range(group):
             for blk in range(blk_count):
                 first = blk * width
                 if first < HALF:
@@ -154,50 +167,60 @@
                 start = one * J + at
                 real = spread(waves[start : start + 8, :K], order)
                 imag = spread(waves[start : start + 8, K:], order)
-                out_ref[blk, step * chunk + one] = jnp.where(real_row, real, imag)
+                made[blk, step * group + one] = jnp.where(real_row, real, imag)
+        part = pl.ds(step * group, group)
+        pltpu.make_async_copy(made.at[:, part], out_ref.at[:, part], moved).start()
+
+    steps = boxes // group
+    legendre(0, 0, first=True)
+    for copy in dft:
+        copy.wait()
+
+    def both(step, carry):
+        azimuths(step - 1, (step - 1) % 2)
+        legendre(step, step % 2)
         return carry
 
-    lax.fori_loop(0, boxes // chunk, azimuths, 0)
-
-
-def shift_kernel(boxes, sub_count, me_ref, place_ref, child_ref, in_ref, cos_ref, sin_ref, out_ref, inverse):
+    lax.fori_loop(1, steps, both, 0)
+    azimuths(steps - 1, (steps - 1) % 2)
+    pltpu.make_async_copy(made, out_ref, moved).wait()
+
+
+def shift_kernel(boxes, sub_count, me_ref, place_ref, child_ref, in_ref, turn_ref, out_ref, made, moved):
     per_peer = boxes // sub_count
     cases = 4
-
-    @pl.when(pl.program_id(0) == 0)
-    def _():
-        for arrival in range(boxes):
-            inverse[place_ref[arrival]] = arrival
-
     even = lax.broadcasted_iota(jnp.int32, (8, K), 0) % 2 == 0
-    count = out_ref.shape[0]
-
-    def one_box(at, carry):
-        box = pl.program_id(0) * count + at
-        arrival = inverse[box]
+    me = me_ref[0]
+
+    def one_box(arrival, carry):
+        box = place_ref[me, arrival]
         source = arrival // per_peer
         rank = arrival % per_peer
         waves = [in_ref[rank * cases + case, source] for case in range(cases)]
         crossed = [jnp.where(even, pltpu.roll(w, 7, 0), pltpu.roll(w, 1, 0)) for w in waves]
         for child in range(8):
             octant = child_ref[box, child]
-            cosine, sine = cos_ref[0, octant], sin_ref[0, octant]
+            cosine, sine = turn_ref[octant, 0], turn_ref[octant, 1]
             for case in range(cases):
-                out_ref[at, case * 8 + child] = waves[case] * cosine + crossed[case] * sine
+                made[arrival, case * 8 + child] = waves[case] * cosine + crossed[case] * sine
+        pltpu.make_async_copy(made.at[arrival], out_ref.at[box], moved).start()
         return carry
 
-    lax.fori_loop(0, count, one_box, 0)
+    lax.fori_loop(0, boxes, one_box, 0, unroll=2)
+    pltpu.make_async_copy(made, out_ref, moved).wait()
 
 
 def body(coefficients, owner_slot, child_list):
     box_count, cases = coefficients.shape[:2]
     sub_count = lax.axis_size("sub")
     blk_count = lax.axis_size("blk")
-    per_peer = box_count // sub_count
     vmem = pl.BlockSpec(memory_space=pltpu.VMEM)
     smem = pl.BlockSpec(memory_space=pltpu.SMEM)
+    anywhere = pl.BlockSpec(memory_space=pl.ANY)
+    near = lambda array: pltpu.with_memory_space_constraint(array, pltpu.VMEM)
+    far = lambda array: pltpu.with_memory_space_constraint(array, pltpu.HBM)
     sub_index = lax.axis_index("sub").reshape(1)
-    blk_index = lax.axis_index("blk").reshape(1)
+    limit = pltpu.CompilerParams(vmem_limit_bytes=16 * 2**20)
 
     outgoing, places = pl.pallas_call(
         lambda *refs: pack_kernel(sub_count, *refs),
@@ -205,12 +228,13 @@
             jax.ShapeDtypeStruct((box_count, cases * 8, M), F32),
             jax.ShapeDtypeStruct((sub_count, box_count), jnp.int32),
         ),
-        in_specs=[smem, smem, vmem],
-        out_specs=(vmem, vmem),
-        scratch_shapes=[pltpu.SMEM((sub_count,), jnp.int32)],
+        in_specs=[smem, smem, anywhere],
+        out_specs=(anywhere, vmem),
+        scratch_shapes=[pltpu.SMEM((sub_count,), jnp.int32), pltpu.SemaphoreType.DMA],
+        compiler_params=limit,
         name="pack",
-    )(sub_index, owner_slot, coefficients.reshape(box_count, cases * 8, M))
-    arrived_places = lax.psum_scatter(places, "sub", scatter_dimension=0, tiled=False)
+    )(sub_index, far(owner_slot), far(coefficients.reshape(box_count, cases * 8, M)))
+    places = lax.psum(places, "sub")
 
     arrived = lax.all_to_all(outgoing.reshape(box_count * cases, 8, M), ("sub", "blk"), 0, 0, tiled=True)
 
@@ -218,32 +242,35 @@
     waves = pl.pallas_call(
         lambda *refs: transform_kernel(blk_count, *refs),
         out_shape=jax.ShapeDtypeStruct((blk_count, sub_count, 8, K), F32),
-        in_specs=[vmem] * 4,
-        out_specs=vmem,
-        scratch_shapes=[pltpu.VMEM((sub_count * J, 2 * M), F32)],
+        in_specs=[vmem] + [anywhere] * 4,
+        out_specs=anywhere,
+        scratch_shapes=[
+            pltpu.VMEM((L, HALF, M), F32),
+            pltpu.VMEM((2 * M, 2 * K), BF16),
+            pltpu.VMEM((2 * M, 2 * K), BF16),
+            pltpu.VMEM((2, 2 * J, 2 * M), F32),
+            pltpu.VMEM((blk_count, sub_count, 8, K), F32),
+            pltpu.SemaphoreType.DMA((4,)),
+            pltpu.SemaphoreType.DMA((2,)),
+            pltpu.SemaphoreType.DMA,
+        ],
+        compiler_params=limit,
         name="transform",
-    )(arrived, jnp.asarray(legendre_half()), jnp.asarray(high), jnp.asarray(rest))
+    )(near(arrived), far(jnp.asarray(legendre_half())), far(jnp.asarray(high)), far(jnp.asarray(rest)), places)
 
     rows = lax.all_to_all(waves, "blk", 0, 0, tiled=True)
 
-    cosine, sine = shift_tables(blk_count)
-    step = 4
+    turns = jnp.asarray(np.stack(shift_tables(blk_count), axis=2))
+    turns = lax.dynamic_index_in_dim(turns, lax.axis_index("blk"), 0, keepdims=False)
     children = pl.pallas_call(
         lambda *refs: shift_kernel(box_count, sub_count, *refs),
         out_shape=jax.ShapeDtypeStruct((box_count, cases * 8, 8, K), F32),
-        grid_spec=pltpu.PrefetchScalarGridSpec(
-            num_scalar_prefetch=3,
-            grid=(box_count // step,),
-            in_specs=[
-                vmem,
-                pl.BlockSpec((1, 8, 8, K), lambda i, me, place, child: (me[0], 0, 0, 0)),
-                pl.BlockSpec((1, 8, 8, K), lambda i, me, place, child: (me[0], 0, 0, 0)),
-            ],
-            out_specs=pl.BlockSpec((step, cases * 8, 8, K), lambda i, me, place, child: (i, 0, 0, 0)),
-            scratch_shapes=[pltpu.SMEM((box_count,), jnp.int32)],
-        ),
+        in_specs=[smem, smem, smem, vmem, vmem],
+        out_specs=anywhere,
+        scratch_shapes=[pltpu.VMEM((box_count, cases * 8, 8, K), F32), pltpu.SemaphoreType.DMA],
+        compiler_params=limit,
         name="shift",
-    )(blk_index, arrived_places, child_list, rows, jnp.asarray(cosine), jnp.asarray(sine))
+    )(sub_index, places, child_list, near(rows), near(turns))
     return children.reshape(box_count, cases, 8, J // blk_count, 2, K)
 
 

time: 87 us -> 118 us (1.36)
  Pallas kernels: 18.5 us -> 43.8 us
  blocking collectives: 58.5 us -> 33.9 us
  starting transfers between devices: 4.93 us -> 23.8 us
  waiting for transfers between devices: 0.87 us -> 14.9 us
  local copies, waits for them, and re-layouts: 3.46 us -> 0.93 us
    all_to_all x1 -> x0, blocking collectives: 46 us -> none  [body(): lax.all_to_all(outgoing.reshape(box_count * cases, 8, M), ('sub', 'blk'),...]
    psum x0 -> x1, blocking collectives: none -> 33.9 us  [body(): places = lax.psum(places, 'sub')]
    pallas_call x1, Pallas kernels: 2.78 us -> 33.7 us  [body(): pl.pallas_call(lambda *refs: pack_kernel(sub_count, *refs), out_shape=(ja...]
    all_to_all x0 -> x1, starting transfers between devices: none -> 15.7 us  [body(): lax.all_to_all(outgoing.reshape(box_count * cases, 8, M), ('sub', 'blk'),...]
    all_to_all x1, waiting for transfers between devices: 0.87 us -> 14.9 us  [body(): rows = lax.all_to_all(waves, 'blk', 0, 0, tiled=True)]
    unnamed x1 -> x0, blocking collectives: 12.5 us -> none
    pallas_call x1, Pallas kernels: 9.85 us -> 4.46 us  [body(): pl.pallas_call(lambda *refs: shift_kernel(box_count, sub_count, *refs), o...]
    all_to_all x1, starting transfers between devices: 4.93 us -> 8.18 us  [body(): rows = lax.all_to_all(waves, 'blk', 0, 0, tiled=True)]
  transfers between devices with their start and end apart: 1 -> 2, of which waited for: 1 -> 1; matrix products, arithmetic and copies ran while one was open for 3% -> 1% of each run, Pallas kernels for 0% -> 0%
where the time goes in v2:
time: 118 us; the launch traced here: 117 us
  Pallas kernels  43.8 us (37%)
  blocking collectives  33.9 us (29%)
  starting transfers between devices  23.8 us (20%)
  waiting for transfers between devices  14.9 us (13%)
    psum x1, blocking collectives, body(): places = lax.psum(places, 'sub')  33.9 us
    pallas_call x1, Pallas kernels, body(): pl.pallas_call(lambda *refs: pack_kernel(sub_count, *refs), out_shape=(ja...  33.7 us
    all_to_all x1, starting transfers between devices, body(): lax.all_to_all(outgoing.reshape(box_count * cases, 8, M), ('sub', 'blk'),...  15.7 us
    all_to_all x1, waiting for transfers between devices, body(): rows = lax.all_to_all(waves, 'blk', 0, 0, tiled=True)  14.9 us
    all_to_all x1, starting transfers between devices, body(): rows = lax.all_to_all(waves, 'blk', 0, 0, tiled=True)  8.18 us
    pallas_call x1, Pallas kernels, body(): pl.pallas_call(lambda *refs: transform_kernel(blk_count, *refs), out_shap...  5.64 us
    pallas_call x1, Pallas kernels, body(): pl.pallas_call(lambda *refs: shift_kernel(box_count, sub_count, *refs), o...  4.46 us
  transfers between devices with their start and end apart: 2, of which 1 were waited for; matrix products, arithmetic and copies ran while one was open for 1% of the time, Pallas kernels for 0%

profile of v2, /device:TPU:1, one launch (start us, length us, event | category | flops | bytes accessed | tf_op | source)
XLA Modules:
  0.0 117.3 jit_solution(4171793733642081822)
XLA Ops:
  0.0 0.0 copy-start
  0.0 33.7 %pack.1 = (f32[64,32,128]{2,1,0:T(8,128)}, s32[16,64]{1,0:T(8,128)S(1)}) custom-call(s32[1]{0:T(128)} %bitcast.refs_0_, s32[64]{0:T(128)} %refs_1_.2, f32[64,32,128]{2,1,0:T(8,128)} %bitcast.6), custom_call_target="tpu_custom_call" | custom-call | tf_op jit(solution)/shard_map/pack/pallas_call | solution.py:225
  33.7 15.7 %all-to-all-start = ((f32[256,8,128]{2,1,0:T(8,128)}), f32[256,8,128]{2,1,0:T(8,128)S(1)}, u32[]{:S(2)}, u32[]{:S(2)}) async-start(f32[256,8,128]{2,1,0:T(8,128)} %bitcast.2), calls=%async_computation | async-start | bytes 2097152 | tf_op jit(solution)/shard_map/all_to_all | solution.py:239
  49.4 33.9 %psum.7.refs_4_.refs_1_ = s32[16,64]{1,0:T(8,128)S(1)} all-reduce(s32[16,64]{1,0:T(8,128)S(1)} %get-tuple-element.7), channel_id=1, replica_groups=mesh['sub'=16,'blk'=16] {'sub'}, use_global_device_ids=true, to_apply=%region_0.0 | all-reduce | flops 1024 | bytes 8192 | tf_op jit(solution)/shard_map/psum | solution.py:237
  83.2 0.0 all-to-all-done.refs_0_
  83.2 5.6 %transform.1 = f32[16,16,8,128]{3,2,1,0:T(8,128)} custom-call(f32[256,8,128]{2,1,0:T(8,128)S(1)} %all-to-all-done.refs_0_, f32[64,32,128]{2,1,0:T(8,128)} %constant.21.clone.refs_1_, bf16[256,256]{1,0:T(8,128)(2,1)} %constant.22.clone.refs_2_, bf16[256,256]{1,0:T(8,128)(2,1)} %constant.23.clone.refs_3_, s32[16,64]{1,0:T(8,128)S(1)} %psum.7.refs_4_.refs_1_), custom_call_target="tpu_custom_call" | custom-call | tf_op jit(solution)/shard_map/transform/pallas_call | solution.py:242
  88.9 8.2 %all-to-all-start.1 = ((f32[16,16,8,128]{3,2,1,0:T(8,128)}), f32[16,16,8,128]{3,2,1,0:T(8,128)S(1)}, u32[]{:S(2)}, u32[]{:S(2)}) async-start(f32[16,16,8,128]{3,2,1,0:T(8,128)} %transform.1), calls=%async_computation.1 | async-start | bytes 2097152 | tf_op jit(solution)/shard_map/all_to_all | solution.py:261
  97.0 0.0 copy-done
  97.0 0.1 copy.8.refs_2_
  97.1 0.8 dynamic-slice_bitcast_fusion.refs_4_
  98.0 14.9 %all-to-all-done.1.refs_3_ = f32[16,16,8,128]{3,2,1,0:T(8,128)S(1)} async-done(((f32[16,16,8,128]{3,2,1,0:T(8,128)}), f32[16,16,8,128]{3,2,1,0:T(8,128)S(1)}, u32[]{:S(2)}, u32[]{:S(2)}) %all-to-all-start.1) | async-done | bytes 1048608 | tf_op jit(solution)/shard_map/all_to_all | solution.py:261
  112.9 4.5 %shift.1 = f32[64,32,8,128]{3,2,1,0:T(8,128)} custom-call(s32[1]{0:T(128)} %bitcast.refs_0_, s32[16,64]{1,0:T(8,128)S(1)} %psum.7.refs_4_.refs_1_, s32[64,8]{1,0:T(8,128)S(1)} %copy.8.refs_2_, f32[16,16,8,128]{3,2,1,0:T(8,128)S(1)} %all-to-all-done.1.refs_3_, f32[8,2,8,128]{3,2,1,0:T(8,128)S(1)} %dynamic-slice_bitcast_fusion.refs_4_), custom_call_target="tpu_custom_call" | custom-call | tf_op jit(solution)/shard_map/shift/pallas_call | solution.py:265
Async XLA Ops:
  0.0 97.0 %copy-start = (s32[64,8]{0,1:T(8,128)S(1)}, s32[64,8]{0,1:T(8,128)}, u32[]{:S(2)}) copy-start(s32[64,8]{0,1:T(8,128)} %param.9) | copy-start | bytes 6148
  33.7 49.5 %all-to-all-start = ((f32[256,8,128]{2,1,0:T(8,128)}), f32[256,8,128]{2,1,0:T(8,128)S(1)}, u32[]{:S(2)}, u32[]{:S(2)}) async-start(f32[256,8,128]{2,1,0:T(8,128)} %bitcast.2), calls=%async_computation | async-start | bytes 2097152 | tf_op jit(solution)/shard_map/all_to_all | solution.py:239
  88.9 24.0 %all-to-all-start.1 = ((f32[16,16,8,128]{3,2,1,0:T(8,128)}), f32[16,16,8,128]{3,2,1,0:T(8,128)S(1)}, u32[]{:S(2)}, u32[]{:S(2)}) async-start(f32[16,16,8,128]{3,2,1,0:T(8,128)} %transform.1), calls=%async_computation.1 | async-start | bytes 2097152 | tf_op jit(solution)/shard_map/all_to_all | solution.py:261

commit v3 on v2

--- a/solution.py
+++ b/solution.py
@@ -71,8 +71,16 @@
     return cut(cosine), cut(sine)
 
 
-def pack_kernel(sub_count, me_ref, slot_ref, coef_ref, out_ref, place_ref, count, moved):
+def pack_kernel(sub_count, me_ref, slot_ref, coef_ref, out_ref, place_ref, held, count, arrived, moved):
     box_count = coef_ref.shape[0]
+    pieces = arrived.shape[0]
+    cut = box_count // pieces
+    arriving = []
+    for piece in range(pieces):
+        part = pl.ds(piece * cut, cut)
+        arriving.append(pltpu.make_async_copy(coef_ref.at[part], held.at[part], arrived.at[piece]))
+    for copy in arriving:
+        copy.start()
     per_peer = box_count // sub_count
     for peer in range(sub_count):
         count[peer] = 0
@@ -81,15 +89,17 @@
     first = me_ref[0] * per_peer
     place = jnp.zeros(place_ref.shape, jnp.int32)
     for box in range(box_count):
+        if box % cut == 0:
+            arriving[box // cut].wait()
         slot = slot_ref[box]
         peer = slot // box_count
         rank = count[peer]
         count[peer] = rank + 1
-        pltpu.make_async_copy(coef_ref.at[box], out_ref.at[peer * per_peer + rank], moved).start()
+        pltpu.make_async_copy(held.at[box], out_ref.at[peer * per_peer + rank], moved).start()
         here = (row == peer) & (lane == first + rank)
         place = jnp.where(here, slot - peer * box_count, place)
     place_ref[...] = place
-    pltpu.make_async_copy(coef_ref, out_ref, moved).wait()
+    pltpu.make_async_copy(held, out_ref, moved).wait()
 
 
 def spread(value, order):
@@ -97,10 +107,9 @@
 
 
 def transform_kernel(
-    blk_count, in_ref, table_hbm, high_hbm, rest_hbm, place_ref, out_ref,
+    blk_count, in_ref, table_hbm, high_hbm, rest_hbm, out_ref,
     table_ref, high_ref, rest_ref, cycles, made, table_in, dft_in, moved,
 ):
-    del place_ref
     pieces = table_in.shape[0]
     cut = L // pieces
     arriving = []
@@ -210,67 +219,96 @@
     pltpu.make_async_copy(made, out_ref, moved).wait()
 
 
-def body(coefficients, owner_slot, child_list):
-    box_count, cases = coefficients.shape[:2]
-    sub_count = lax.axis_size("sub")
-    blk_count = lax.axis_size("blk")
-    vmem = pl.BlockSpec(memory_space=pltpu.VMEM)
-    smem = pl.BlockSpec(memory_space=pltpu.SMEM)
-    anywhere = pl.BlockSpec(memory_space=pl.ANY)
-    near = lambda array: pltpu.with_memory_space_constraint(array, pltpu.VMEM)
-    far = lambda array: pltpu.with_memory_space_constraint(array, pltpu.HBM)
-    sub_index = lax.axis_index("sub").reshape(1)
-    limit = pltpu.CompilerParams(vmem_limit_bytes=16 * 2**20)
-
-    outgoing, places = pl.pallas_call(
+def whole(space):
+    return pl.BlockSpec(memory_space=space)
+
+
+def limit(mebibytes):
+    return pltpu.CompilerParams(vmem_limit_bytes=mebibytes * 2**20)
+
+
+def near(array):
+    return pltpu.with_memory_space_constraint(array, pltpu.VMEM)
+
+
+def far(array):
+    return pltpu.with_memory_space_constraint(array, pltpu.HBM)
+
+
+def pack(sub_index, owner_slot, coefficients, sub_count):
+    box_count = coefficients.shape[0]
+    shape = (box_count, coefficients.size // (box_count * M), M)
+    return pl.pallas_call(
         lambda *refs: pack_kernel(sub_count, *refs),
         out_shape=(
-            jax.ShapeDtypeStruct((box_count, cases * 8, M), F32),
+            jax.ShapeDtypeStruct(shape, F32),
             jax.ShapeDtypeStruct((sub_count, box_count), jnp.int32),
         ),
-        in_specs=[smem, smem, anywhere],
-        out_specs=(anywhere, vmem),
-        scratch_shapes=[pltpu.SMEM((sub_count,), jnp.int32), pltpu.SemaphoreType.DMA],
-        compiler_params=limit,
+        in_specs=[whole(pltpu.SMEM), whole(pltpu.SMEM), whole(pl.ANY)],
+        out_specs=(whole(pl.ANY), whole(pltpu.VMEM)),
+        scratch_shapes=[
+            pltpu.VMEM(shape, F32),
+            pltpu.SMEM((sub_count,), jnp.int32),
+            pltpu.SemaphoreType.DMA((4,)),
+            pltpu.SemaphoreType.DMA,
+        ],
+        compiler_params=limit(16),
         name="pack",
-    )(sub_index, far(owner_slot), far(coefficients.reshape(box_count, cases * 8, M)))
-    places = lax.psum(places, "sub")
-
-    arrived = lax.all_to_all(outgoing.reshape(box_count * cases, 8, M), ("sub", "blk"), 0, 0, tiled=True)
-
+    )(sub_index, far(owner_slot), far(coefficients.reshape(shape)))
+
+
+def transform(arrived, blk_count):
+    boxes = arrived.shape[0] // blk_count
     high, rest = dft_halves()
-    waves = pl.pallas_call(
+    made = (blk_count, boxes, 8, K)
+    return pl.pallas_call(
         lambda *refs: transform_kernel(blk_count, *refs),
-        out_shape=jax.ShapeDtypeStruct((blk_count, sub_count, 8, K), F32),
-        in_specs=[vmem] + [anywhere] * 4,
-        out_specs=anywhere,
+        out_shape=jax.ShapeDtypeStruct(made, F32),
+        in_specs=[whole(pltpu.VMEM)] + [whole(pl.ANY)] * 3,
+        out_specs=whole(pl.ANY),
         scratch_shapes=[
             pltpu.VMEM((L, HALF, M), F32),
             pltpu.VMEM((2 * M, 2 * K), BF16),
             pltpu.VMEM((2 * M, 2 * K), BF16),
             pltpu.VMEM((2, 2 * J, 2 * M), F32),
-            pltpu.VMEM((blk_count, sub_count, 8, K), F32),
+            pltpu.VMEM(made, F32),
             pltpu.SemaphoreType.DMA((4,)),
             pltpu.SemaphoreType.DMA((2,)),
             pltpu.SemaphoreType.DMA,
         ],
-        compiler_params=limit,
+        compiler_params=limit(16),
         name="transform",
-    )(near(arrived), far(jnp.asarray(legendre_half())), far(jnp.asarray(high)), far(jnp.asarray(rest)), places)
-
+    )(near(arrived), far(jnp.asarray(legendre_half())), far(jnp.asarray(high)), far(jnp.asarray(rest)))
+
+
+def shift(sub_index, places, child_list, rows, turns):
+    sub_count, boxes = places.shape
+    cases = rows.shape[0] * sub_count // boxes
+    shape = (boxes, cases * 8, 8, K)
+    return pl.pallas_call(
+        lambda *refs: shift_kernel(boxes, sub_count, *refs),
+        out_shape=jax.ShapeDtypeStruct(shape, F32),
+        in_specs=[whole(pltpu.SMEM)] * 3 + [whole(pltpu.VMEM)] * 2,
+        out_specs=whole(pl.ANY),
+        scratch_shapes=[pltpu.VMEM(shape, F32), pltpu.SemaphoreType.DMA],
+        compiler_params=limit(16),
+        name="shift",
+    )(sub_index, places, child_list, near(rows), near(turns))
+
+
+def body(coefficients, owner_slot, child_list):
+    box_count, cases = coefficients.shape[:2]
+    blk_count = lax.axis_size("blk")
+    sub_index = lax.axis_index("sub").reshape(1)
+
+    outgoing, places = pack(sub_index, owner_slot, coefficients, lax.axis_size("sub"))
+    arrived = lax.all_to_all(outgoing.reshape(box_count * cases, 8, M), ("sub", "blk"), 0, 0, tiled=True)
+    waves = transform(arrived, blk_count)
     rows = lax.all_to_all(waves, "blk", 0, 0, tiled=True)
-
+    places = lax.psum(places, "sub")
     turns = jnp.asarray(np.stack(shift_tables(blk_count), axis=2))
     turns = lax.dynamic_index_in_dim(turns, lax.axis_index("blk"), 0, keepdims=False)
-    children = pl.pallas_call(
-        lambda *refs: shift_kernel(box_count, sub_count, *refs),
-        out_shape=jax.ShapeDtypeStruct((box_count, cases * 8, 8, K), F32),
-        in_specs=[smem, smem, smem, vmem, vmem],
-        out_specs=anywhere,
-        scratch_shapes=[pltpu.VMEM((box_count, cases * 8, 8, K), F32), pltpu.SemaphoreType.DMA],
-        compiler_params=limit,
-        name="shift",
-    )(sub_index, places, child_list, near(rows), near(turns))
+    children = shift(sub_index, places, child_list, rows, turns)
     return children.reshape(box_count, cases, 8, J // blk_count, 2, K)
 
 

time: 118 us -> 80.9 us (0.69)
  Pallas kernels: 43.8 us -> 14.1 us
  blocking collectives: 33.9 us -> 59.4 us
  starting transfers between devices: 23.8 us -> 4.94 us
  waiting for transfers between devices: 14.9 us -> 1.21 us
    all_to_all x0 -> x1, blocking collectives: none -> 45.7 us  [body(): lax.all_to_all(outgoing.reshape(box_count * cases, 8, M), ('sub', 'blk'),...]
    pallas_call x3, Pallas kernels: 43.8 us -> 14.1 us  [the longest x1 5.64 us: transform(): pl.pallas_call(lambda *refs: transform_kernel(blk_count, *refs), out_shap...]
    psum x1, blocking collectives: 33.9 us -> 13.8 us  [body(): places = lax.psum(places, 'sub')]
    all_to_all x1 -> x0, starting transfers between devices: 15.7 us -> none  [body(): lax.all_to_all(outgoing.reshape(box_count * cases, 8, M), ('sub', 'blk'),...]
    all_to_all x1, waiting for transfers between devices: 14.9 us -> 1.21 us  [body(): rows = lax.all_to_all(waves, 'blk', 0, 0, tiled=True)]
    all_to_all x1, starting transfers between devices: 8.18 us -> 4.94 us  [body(): rows = lax.all_to_all(waves, 'blk', 0, 0, tiled=True)]
  transfers between devices with their start and end apart: 2 -> 1, of which waited for: 1 -> 1; matrix products, arithmetic and copies ran while one was open for 1% -> 1% of each run, Pallas kernels for 0% -> 0%
where the time goes in v3:
time: 80.9 us; the launch traced here: 80.6 us
  blocking collectives  59.4 us (73%)
  Pallas kernels  14.1 us (17%)
  starting transfers between devices  4.94 us (6%)
  waiting for transfers between devices  1.21 us (1%)
  local copies, waits for them, and re-layouts  0.93 us (1%)
    all_to_all x1, blocking collectives, body(): lax.all_to_all(outgoing.reshape(box_count * cases, 8, M), ('sub', 'blk'),...  45.7 us
    psum x1, blocking collectives, body(): places = lax.psum(places, 'sub')  13.8 us
    pallas_call x1, Pallas kernels, transform(): pl.pallas_call(lambda *refs: transform_kernel(blk_count, *refs), out_shap...  5.64 us
    all_to_all x1, starting transfers between devices, body(): rows = lax.all_to_all(waves, 'blk', 0, 0, tiled=True)  4.94 us
    pallas_call x1, Pallas kernels, shift(): pl.pallas_call(lambda *refs: shift_kernel(boxes, sub_count, *refs), out_s...  4.46 us
    pallas_call x1, Pallas kernels, pack(): pl.pallas_call(lambda *refs: pack_kernel(sub_count, *refs), out_shape=(ja...  3.97 us
  transfers between devices with their start and end apart: 1, of which 1 were waited for; matrix products, arithmetic and copies ran while one was open for 1% of the time, Pallas kernels for 0%

profile of v3, /device:TPU:1, one launch (start us, length us, event | category | flops | bytes accessed | tf_op | source)
XLA Modules:
  0.0 80.6 jit_solution(842592041721582073)
XLA Ops:
  0.0 0.0 copy-start
  0.0 4.0 %pack.1 = (f32[64,32,128]{2,1,0:T(8,128)S(1)}, s32[16,64]{1,0:T(8,128)S(1)}) custom-call(s32[1]{0:T(128)} %bitcast.refs_0_, s32[64]{0:T(128)} %refs_1_.2, f32[64,32,128]{2,1,0:T(8,128)} %bitcast.7), custom_call_target="tpu_custom_call" | custom-call | tf_op jit(solution)/shard_map/pack/pallas_call | solution.py:241
  4.0 45.7 %all_to_all.10.refs_0_ = f32[256,8,128]{2,1,0:T(8,128)S(1)} all-to-all(f32[256,8,128]{2,1,0:T(8,128)S(1)} %bitcast.6), channel_id=1, replica_groups=mesh['sub'=16,'blk'=16] {'sub','blk'}, dimensions={0} | all-to-all | bytes 2097152 | tf_op jit(solution)/shard_map/all_to_all | solution.py:305
  49.7 5.6 %transform.1 = f32[16,16,8,128]{3,2,1,0:T(8,128)} custom-call(f32[256,8,128]{2,1,0:T(8,128)S(1)} %all_to_all.10.refs_0_, f32[64,32,128]{2,1,0:T(8,128)} %constant.21.clone.refs_1_, bf16[256,256]{1,0:T(8,128)(2,1)} %constant.22.clone.refs_2_, bf16[256,256]{1,0:T(8,128)(2,1)} %constant.23.clone.refs_3_), custom_call_target="tpu_custom_call" | custom-call | tf_op jit(solution)/shard_map/transform/pallas_call | solution.py:264
  55.3 4.9 %all-to-all-start.1 = ((f32[16,16,8,128]{3,2,1,0:T(8,128)}), f32[16,16,8,128]{3,2,1,0:T(8,128)S(1)}, u32[]{:S(2)}, u32[]{:S(2)}) async-start(f32[16,16,8,128]{3,2,1,0:T(8,128)} %transform.1), calls=%async_computation.1 | async-start | bytes 2097152 | tf_op jit(solution)/shard_map/all_to_all | solution.py:307
  60.2 0.0 copy-done
  60.3 0.1 copy.8.refs_2_
  60.3 13.8 %psum.7.refs_1_ = s32[16,64]{1,0:T(8,128)S(1)} all-reduce(s32[16,64]{1,0:T(8,128)S(1)} %get-tuple-element.7), channel_id=1, replica_groups=mesh['sub'=16,'blk'=16] {'sub'}, use_global_device_ids=true, to_apply=%region_0.0 | all-reduce | flops 1024 | bytes 8192 | tf_op jit(solution)/shard_map/psum | solution.py:308
  74.1 0.8 %dynamic-slice_bitcast_fusion.refs_4_ = f32[8,2,8,128]{3,2,1,0:T(8,128)S(1)} fusion(f32[16,8,2,8,128]{4,3,2,1,0:T(8,128)} %constant.24.clone, s32[]{:T(128)S(6)} %select_n.4), kind=kLoop, calls=%fused_computation | loop fusion | bytes 131076 | tf_op jit(solution)/shard_map/jit(dynamic_index_in_dim)/squeeze | solution.py:310
  74.9 1.2 %all-to-all-done.1.refs_3_ = f32[16,16,8,128]{3,2,1,0:T(8,128)S(1)} async-done(((f32[16,16,8,128]{3,2,1,0:T(8,128)}), f32[16,16,8,128]{3,2,1,0:T(8,128)S(1)}, u32[]{:S(2)}, u32[]{:S(2)}) %all-to-all-start.1) | async-done | bytes 1048608 | tf_op jit(solution)/shard_map/all_to_all | solution.py:307
  76.2 4.5 %shift.1 = f32[64,32,8,128]{3,2,1,0:T(8,128)} custom-call(s32[1]{0:T(128)} %bitcast.refs_0_, s32[16,64]{1,0:T(8,128)S(1)} %psum.7.refs_1_, s32[64,8]{1,0:T(8,128)S(1)} %copy.8.refs_2_, f32[16,16,8,128]{3,2,1,0:T(8,128)S(1)} %all-to-all-done.1.refs_3_, f32[8,2,8,128]{3,2,1,0:T(8,128)S(1)} %dynamic-slice_bitcast_fusion.refs_4_), custom_call_target="tpu_custom_call" | custom-call | tf_op jit(solution)/shard_map/shift/pallas_call | solution.py:288
Async XLA Ops:
  0.0 60.3 %copy-start = (s32[64,8]{0,1:T(8,128)S(1)}, s32[64,8]{0,1:T(8,128)}, u32[]{:S(2)}) copy-start(s32[64,8]{0,1:T(8,128)} %param.9) | copy-start | bytes 6148
  55.3 20.8 %all-to-all-start.1 = ((f32[16,16,8,128]{3,2,1,0:T(8,128)}), f32[16,16,8,128]{3,2,1,0:T(8,128)S(1)}, u32[]{:S(2)}, u32[]{:S(2)}) async-start(f32[16,16,8,128]{3,2,1,0:T(8,128)} %transform.1), calls=%async_computation.1 | async-start | bytes 2097152 | tf_op jit(solution)/shard_map/all_to_all | solution.py:307

commit v4 on v3

--- a/solution.py
+++ b/solution.py
@@ -71,57 +71,65 @@
     return cut(cosine), cut(sine)
 
 
-def pack_kernel(sub_count, me_ref, slot_ref, coef_ref, out_ref, place_ref, held, count, arrived, moved):
-    box_count = coef_ref.shape[0]
-    pieces = arrived.shape[0]
+def pack_kernel(sub_count, slot_hbm, coef_hbm, out_ref, place_ref, slot_ref, held, slot_in, coef_in):
+    box_count = coef_hbm.shape[0]
+    per_peer = box_count // sub_count
+    pieces = coef_in.shape[0]
     cut = box_count // pieces
+    slots = pltpu.make_async_copy(slot_hbm, slot_ref, slot_in)
+    slots.start()
     arriving = []
     for piece in range(pieces):
         part = pl.ds(piece * cut, cut)
-        arriving.append(pltpu.make_async_copy(coef_ref.at[part], held.at[part], arrived.at[piece]))
+        arriving.append(pltpu.make_async_copy(coef_hbm.at[part], held.at[part], coef_in.at[piece]))
     for copy in arriving:
         copy.start()
-    per_peer = box_count // sub_count
-    for peer in range(sub_count):
-        count[peer] = 0
     row = lax.broadcasted_iota(jnp.int32, place_ref.shape, 0)
     lane = lax.broadcasted_iota(jnp.int32, place_ref.shape, 1)
-    first = me_ref[0] * per_peer
+    key = row * box_count + lane - lax.axis_index("sub") * per_peer
     place = jnp.zeros(place_ref.shape, jnp.int32)
+    half = sub_count // 2
+    counts = [jnp.int32(0), jnp.int32(0)]
+    ranks = []
+    slots.wait()
+    for box in range(box_count):
+        slot = slot_ref[box]
+        peer = slot // box_count
+        second = peer >= half
+        shift_by = (peer % half) * 4
+        word = jnp.where(second, counts[1], counts[0])
+        rank = (word >> shift_by) & 7
+        word = word + (jnp.int32(1) << shift_by)
+        counts = [jnp.where(second, counts[0], word), jnp.where(second, word, counts[1])]
+        place = jnp.where(key == peer * box_count + rank, slot % box_count, place)
+        ranks.append(peer * per_peer + rank)
+    place_ref[...] = place
     for box in range(box_count):
         if box % cut == 0:
             arriving[box // cut].wait()
-        slot = slot_ref[box]
-        peer = slot // box_count
-        rank = count[peer]
-        count[peer] = rank + 1
-        pltpu.make_async_copy(held.at[box], out_ref.at[peer * per_peer + rank], moved).start()
-        here = (row == peer) & (lane == first + rank)
-        place = jnp.where(here, slot - peer * box_count, place)
-    place_ref[...] = place
-    pltpu.make_async_copy(held, out_ref, moved).wait()
+        out_ref[ranks[box]] = held[box]
+
+
+def stage_kernel(table_hbm, high_hbm, rest_hbm, turn_hbm, place_ref, table_ref, high_ref, rest_ref, turn_ref, moved):
+    del place_ref
+    pairs = [
+        (table_hbm, table_ref),
+        (high_hbm, high_ref),
+        (rest_hbm, rest_ref),
+        (turn_hbm.at[lax.axis_index("blk")], turn_ref),
+    ]
+    copies = [pltpu.make_async_copy(source, target, moved.at[at]) for at, (source, target) in enumerate(pairs)]
+    for copy in copies:
+        copy.start()
+    for copy in copies:
+        copy.wait()
 
 
 def spread(value, order):
     return jnp.take_along_axis(value, order, axis=0)
 
 
-def transform_kernel(
-    blk_count, in_ref, table_hbm, high_hbm, rest_hbm, out_ref,
-    table_ref, high_ref, rest_ref, cycles, made, table_in, dft_in, moved,
-):
-    pieces = table_in.shape[0]
-    cut = L // pieces
-    arriving = []
-    for piece in range(pieces):
-        part = pl.ds(piece * cut, cut)
-        arriving.append(pltpu.make_async_copy(table_hbm.at[part], table_ref.at[part], table_in.at[piece]))
-    dft = [
-        pltpu.make_async_copy(high_hbm, high_ref, dft_in.at[0]),
-        pltpu.make_async_copy(rest_hbm, rest_ref, dft_in.at[1]),
-    ]
-    for copy in arriving + dft:
-        copy.start()
+def transform_kernel(blk_count, in_ref, table_ref, high_ref, rest_ref, out_ref, cycles, made, moved):
     boxes = in_ref.shape[0] // blk_count
     degrees = L // blk_count
     group = 2
@@ -129,12 +137,10 @@
     lane = lax.broadcasted_iota(jnp.int32, (8, M), 1)
     mirror = jnp.where(lane % 2 == 0, 1.0, -1.0).astype(F32)
 
-    def legendre(step, slot, first=False):
+    def legendre(step, slot):
         sums = [[[None] * vregs for _ in range(2)] for _ in range(2 * group)]
         for degree in range(L):
             source, row = degree // degrees, degree % degrees
-            if first and degree % cut == 0:
-                arriving[degree // cut].wait()
             table = [table_ref[degree, 8 * v : 8 * v + 8, :] for v in range(vregs)]
             for one in range(2 * group):
                 box, part = step * group + one // 2, one % 2
@@ -181,25 +187,19 @@
         pltpu.make_async_copy(made.at[:, part], out_ref.at[:, part], moved).start()
 
     steps = boxes // group
-    legendre(0, 0, first=True)
-    for copy in dft:
-        copy.wait()
-
-    def both(step, carry):
+    legendre(0, 0)
+    for step in range(1, steps):
         azimuths(step - 1, (step - 1) % 2)
         legendre(step, step % 2)
-        return carry
-
-    lax.fori_loop(1, steps, both, 0)
     azimuths(steps - 1, (steps - 1) % 2)
     pltpu.make_async_copy(made, out_ref, moved).wait()
 
 
-def shift_kernel(boxes, sub_count, me_ref, place_ref, child_ref, in_ref, turn_ref, out_ref, made, moved):
+def shift_kernel(boxes, sub_count, place_ref, child_ref, in_ref, turn_ref, out_ref, made, moved):
     per_peer = boxes // sub_count
     cases = 4
     even = lax.broadcasted_iota(jnp.int32, (8, K), 0) % 2 == 0
-    me = me_ref[0]
+    me = lax.axis_index("sub")
 
     def one_box(arrival, carry):
         box = place_ref[me, arrival]
@@ -235,80 +235,86 @@
     return pltpu.with_memory_space_constraint(array, pltpu.HBM)
 
 
-def pack(sub_index, owner_slot, coefficients, sub_count):
+def pack(owner_slot, coefficients, sub_count):
     box_count = coefficients.shape[0]
     shape = (box_count, coefficients.size // (box_count * M), M)
     return pl.pallas_call(
         lambda *refs: pack_kernel(sub_count, *refs),
-        out_shape=(
-            jax.ShapeDtypeStruct(shape, F32),
-            jax.ShapeDtypeStruct((sub_count, box_count), jnp.int32),
-        ),
-        in_specs=[whole(pltpu.SMEM), whole(pltpu.SMEM), whole(pl.ANY)],
-        out_specs=(whole(pl.ANY), whole(pltpu.VMEM)),
+        out_shape=(pltpu.VMEM(shape, F32), jax.ShapeDtypeStruct((sub_count, box_count), jnp.int32)),
+        in_specs=[whole(pl.ANY)] * 2,
+        out_specs=(whole(pltpu.VMEM), whole(pltpu.VMEM)),
         scratch_shapes=[
+            pltpu.SMEM((box_count,), jnp.int32),
             pltpu.VMEM(shape, F32),
-            pltpu.SMEM((sub_count,), jnp.int32),
+            pltpu.SemaphoreType.DMA,
             pltpu.SemaphoreType.DMA((4,)),
-            pltpu.SemaphoreType.DMA,
         ],
         compiler_params=limit(16),
         name="pack",
-    )(sub_index, far(owner_slot), far(coefficients.reshape(shape)))
-
-
-def transform(arrived, blk_count):
+    )(far(owner_slot), far(coefficients.reshape(shape)))
+
+
+def stage(places, blk_count):
+    high, rest = dft_halves()
+    tables = [legendre_half(), high, rest, np.stack(shift_tables(blk_count), axis=2)]
+    tables = [jnp.asarray(table) for table in tables]
+    shapes = [table.shape for table in tables[:3]] + [tables[3].shape[1:]]
+    return pl.pallas_call(
+        stage_kernel,
+        out_shape=[pltpu.VMEM(shape, table.dtype) for shape, table in zip(shapes, tables)],
+        in_specs=[whole(pl.ANY)] * 5,
+        out_specs=[whole(pltpu.VMEM)] * 4,
+        scratch_shapes=[pltpu.SemaphoreType.DMA((4,))],
+        compiler_params=limit(4),
+        cost_estimate=pl.CostEstimate(flops=0, bytes_accessed=4 * 2**20, transcendentals=0),
+        name="stage",
+    )(*[far(table) for table in tables], places)
+
+
+def transform(arrived, table, high, rest, blk_count):
     boxes = arrived.shape[0] // blk_count
-    high, rest = dft_halves()
     made = (blk_count, boxes, 8, K)
     return pl.pallas_call(
         lambda *refs: transform_kernel(blk_count, *refs),
         out_shape=jax.ShapeDtypeStruct(made, F32),
-        in_specs=[whole(pltpu.VMEM)] + [whole(pl.ANY)] * 3,
+        in_specs=[whole(pltpu.VMEM)] * 4,
         out_specs=whole(pl.ANY),
         scratch_shapes=[
-            pltpu.VMEM((L, HALF, M), F32),
-            pltpu.VMEM((2 * M, 2 * K), BF16),
-            pltpu.VMEM((2 * M, 2 * K), BF16),
             pltpu.VMEM((2, 2 * J, 2 * M), F32),
             pltpu.VMEM(made, F32),
-            pltpu.SemaphoreType.DMA((4,)),
-            pltpu.SemaphoreType.DMA((2,)),
             pltpu.SemaphoreType.DMA,
         ],
         compiler_params=limit(16),
         name="transform",
-    )(near(arrived), far(jnp.asarray(legendre_half())), far(jnp.asarray(high)), far(jnp.asarray(rest)))
-
-
-def shift(sub_index, places, child_list, rows, turns):
+    )(near(arrived), near(table), near(high), near(rest))
+
+
+def shift(places, child_list, rows, turns):
     sub_count, boxes = places.shape
     cases = rows.shape[0] * sub_count // boxes
     shape = (boxes, cases * 8, 8, K)
     return pl.pallas_call(
         lambda *refs: shift_kernel(boxes, sub_count, *refs),
         out_shape=jax.ShapeDtypeStruct(shape, F32),
-        in_specs=[whole(pltpu.SMEM)] * 3 + [whole(pltpu.VMEM)] * 2,
+        in_specs=[whole(pltpu.SMEM)] * 2 + [whole(pltpu.VMEM)] * 2,
         out_specs=whole(pl.ANY),
         scratch_shapes=[pltpu.VMEM(shape, F32), pltpu.SemaphoreType.DMA],
         compiler_params=limit(16),
         name="shift",
-    )(sub_index, places, child_list, near(rows), near(turns))
+    )(places, child_list, near(rows), near(turns))
 
 
 def body(coefficients, owner_slot, child_list):
     box_count, cases = coefficients.shape[:2]
     blk_count = lax.axis_size("blk")
-    sub_index = lax.axis_index("sub").reshape(1)
-
-    outgoing, places = pack(sub_index, owner_slot, coefficients, lax.axis_size("sub"))
+
+    outgoing, places = pack(owner_slot, coefficients, lax.axis_size("sub"))
     arrived = lax.all_to_all(outgoing.reshape(box_count * cases, 8, M), ("sub", "blk"), 0, 0, tiled=True)
-    waves = transform(arrived, blk_count)
+    table, high, rest, turns = stage(places, blk_count)
+    waves = transform(arrived, table, high, rest, blk_count)
     rows = lax.all_to_all(waves, "blk", 0, 0, tiled=True)
     places = lax.psum(places, "sub")
-    turns = jnp.asarray(np.stack(shift_tables(blk_count), axis=2))
-    turns = lax.dynamic_index_in_dim(turns, lax.axis_index("blk"), 0, keepdims=False)
-    children = shift(sub_index, places, child_list, rows, turns)
+    children = shift(places, child_list, rows, turns)
     return children.reshape(box_count, cases, 8, J // blk_count, 2, K)
 
 

time: 80.9 us -> 77.9 us (0.963)
  blocking collectives: 59.4 us -> 13.8 us
  waiting for transfers between devices: 1.21 us -> 31 us
  starting transfers between devices: 4.94 us -> 20.6 us
  Pallas kernels: 14.1 us -> 12.2 us
  local copies, waits for them, and re-layouts: 0.93 us -> 0.09 us
    all_to_all x1 -> x0, blocking collectives: 45.7 us -> none  [body(): lax.all_to_all(outgoing.reshape(box_count * cases, 8, M), ('sub', 'blk'),...]
    all_to_all x0 -> x1, waiting for transfers between devices: none -> 28.9 us  [body(): lax.all_to_all(outgoing.reshape(box_count * cases, 8, M), ('sub', 'blk'),...]
    all_to_all x0 -> x1, starting transfers between devices: none -> 15.7 us  [body(): lax.all_to_all(outgoing.reshape(box_count * cases, 8, M), ('sub', 'blk'),...]
    pallas_call x1, Pallas kernels: 5.64 us -> 3.68 us  [transform(): pl.pallas_call(lambda *refs: transform_kernel(blk_count, *refs), out_shap...]
    all_to_all x1, waiting for transfers between devices: 1.21 us -> 2.06 us  [body(): rows = lax.all_to_all(waves, 'blk', 0, 0, tiled=True)]
    squeeze x1 -> x0, local copies, waits for them, and re-layouts: 0.84 us -> none  [body(): lax.dynamic_index_in_dim(turns, lax.axis_index('blk'), 0, keepdims=False)]
    pallas_call x1 -> x2, Pallas kernels: 3.97 us -> 4.06 us  [the longest x1 2.76 us: pack(): pl.pallas_call(lambda *refs: pack_kernel(sub_count, *refs), out_shape=(pl...]
  transfers between devices with their start and end apart: 1 -> 2, of which waited for: 1 -> 2; matrix products, arithmetic and copies ran while one was open for 1% -> 0% of each run, Pallas kernels for 0% -> 2%
where the time goes in v4:
time: 77.9 us; the launch traced here: 77.7 us
  waiting for transfers between devices  31 us (40%)
  starting transfers between devices  20.6 us (26%)
  blocking collectives  13.8 us (18%)
  Pallas kernels  12.2 us (16%)
    all_to_all x1, waiting for transfers between devices, body(): lax.all_to_all(outgoing.reshape(box_count * cases, 8, M), ('sub', 'blk'),...  28.9 us
    all_to_all x1, starting transfers between devices, body(): lax.all_to_all(outgoing.reshape(box_count * cases, 8, M), ('sub', 'blk'),...  15.7 us
    psum x1, blocking collectives, body(): places = lax.psum(places, 'sub')  13.8 us
    all_to_all x1, starting transfers between devices, body(): rows = lax.all_to_all(waves, 'blk', 0, 0, tiled=True)  4.94 us
    pallas_call x1, Pallas kernels, shift(): pl.pallas_call(lambda *refs: shift_kernel(boxes, sub_count, *refs), out_s...  4.47 us
    pallas_call x1, Pallas kernels, transform(): pl.pallas_call(lambda *refs: transform_kernel(blk_count, *refs), out_shap...  3.68 us
    pallas_call x1, Pallas kernels, pack(): pl.pallas_call(lambda *refs: pack_kernel(sub_count, *refs), out_shape=(pl...  2.76 us
    all_to_all x1, waiting for transfers between devices, body(): rows = lax.all_to_all(waves, 'blk', 0, 0, tiled=True)  2.06 us
  transfers between devices with their start and end apart: 2, of which 2 were waited for; matrix products, arithmetic and copies ran while one was open for 0% of the time, Pallas kernels for 2%

profile of v4, /device:TPU:1, one launch (start us, length us, event | category | flops | bytes accessed | tf_op | source)
XLA Modules:
  0.0 77.7 jit_solution(15249053050491275980)
XLA Ops:
  0.0 0.0 copy-start
  0.0 2.8 %pack.1 = (f32[64,32,128]{2,1,0:T(8,128)}, s32[16,64]{1,0:T(8,128)S(1)}) custom-call(s32[64]{0:T(128)} %refs_0_.1, f32[64,32,128]{2,1,0:T(8,128)} %bitcast.3), custom_call_target="tpu_custom_call" | custom-call | tf_op jit(solution)/shard_map/pack/pallas_call | solution.py:241
  2.8 15.7 %all-to-all-start = ((f32[256,8,128]{2,1,0:T(8,128)}), f32[256,8,128]{2,1,0:T(8,128)S(1)}, u32[]{:S(2)}, u32[]{:S(2)}) async-start(f32[256,8,128]{2,1,0:T(8,128)} %bitcast.1), calls=%async_computation | async-start | bytes 2097152 | tf_op jit(solution)/shard_map/all_to_all | solution.py:312
  18.4 1.3 %stage.1 = (f32[64,32,128]{2,1,0:T(8,128)S(1)}, bf16[256,256]{1,0:T(8,128)(2,1)S(1)}, bf16[256,256]{1,0:T(8,128)(2,1)S(1)}, f32[8,2,8,128]{3,2,1,0:T(8,128)S(1)}) custom-call(f32[64,32,128]{2,1,0:T(8,128)} %constant.8.clone.table_hbm, bf16[256,256]{1,0:T(8,128)(2,1)} %constant.9.clone.high_hbm, bf16[256,256]{1,0:T(8,128)(2,1)} %constant.10.clone.rest_hbm, ...), custom_call_target="tpu_custom_call" | custom-call | bytes 4194304 | tf_op jit(solution)/shard_map/stage/pallas_call | solution.py:262
  19.7 28.9 %all-to-all-done.refs_0_ = f32[256,8,128]{2,1,0:T(8,128)S(1)} async-done(((f32[256,8,128]{2,1,0:T(8,128)}), f32[256,8,128]{2,1,0:T(8,128)S(1)}, u32[]{:S(2)}, u32[]{:S(2)}) %all-to-all-start) | async-done | bytes 1048608 | tf_op jit(solution)/shard_map/all_to_all | solution.py:312
  48.7 3.7 %transform.1 = f32[16,16,8,128]{3,2,1,0:T(8,128)} custom-call(f32[256,8,128]{2,1,0:T(8,128)S(1)} %all-to-all-done.refs_0_, f32[64,32,128]{2,1,0:T(8,128)S(1)} %get-tuple-element.13.refs_1_, bf16[256,256]{1,0:T(8,128)(2,1)S(1)} %get-tuple-element.14.refs_2_, bf16[256,256]{1,0:T(8,128)(2,1)S(1)} %get-tuple-element.15.refs_3_), custom_call_target="tpu_custom_call" | custom-call | tf_op jit(solution)/shard_map/transform/pallas_call | solution.py:277
  52.3 4.9 %all-to-all-start.1 = ((f32[16,16,8,128]{3,2,1,0:T(8,128)}), f32[16,16,8,128]{3,2,1,0:T(8,128)S(1)}, u32[]{:S(2)}, u32[]{:S(2)}) async-start(f32[16,16,8,128]{3,2,1,0:T(8,128)} %transform.1), calls=%async_computation.1 | async-start | bytes 2097152 | tf_op jit(solution)/shard_map/all_to_all | solution.py:315
  57.3 0.0 copy-done
  57.3 0.1 copy.8.refs_1_
  57.4 13.8 %psum.7.refs_0_ = s32[16,64]{1,0:T(8,128)S(1)} all-reduce(s32[16,64]{1,0:T(8,128)S(1)} %get-tuple-element.11.place_ref), channel_id=1, replica_groups=mesh['sub'=16,'blk'=16] {'sub'}, use_global_device_ids=true, to_apply=%region_0.0 | all-reduce | flops 1024 | bytes 8192 | tf_op jit(solution)/shard_map/psum | solution.py:316
  71.1 2.1 %all-to-all-done.1.refs_2_ = f32[16,16,8,128]{3,2,1,0:T(8,128)S(1)} async-done(((f32[16,16,8,128]{3,2,1,0:T(8,128)}), f32[16,16,8,128]{3,2,1,0:T(8,128)S(1)}, u32[]{:S(2)}, u32[]{:S(2)}) %all-to-all-start.1) | async-done | bytes 1048608 | tf_op jit(solution)/shard_map/all_to_all | solution.py:315
  73.2 4.5 %shift.1 = f32[64,32,8,128]{3,2,1,0:T(8,128)} custom-call(s32[16,64]{1,0:T(8,128)S(1)} %psum.7.refs_0_, s32[64,8]{1,0:T(8,128)S(1)} %copy.8.refs_1_, f32[16,16,8,128]{3,2,1,0:T(8,128)S(1)} %all-to-all-done.1.refs_2_, f32[8,2,8,128]{3,2,1,0:T(8,128)S(1)} %get-tuple-element.16.refs_3_), custom_call_target="tpu_custom_call" | custom-call | tf_op jit(solution)/shard_map/shift/pallas_call | solution.py:296
Async XLA Ops:
  0.0 57.3 %copy-start = (s32[64,8]{0,1:T(8,128)S(1)}, s32[64,8]{0,1:T(8,128)}, u32[]{:S(2)}) copy-start(s32[64,8]{0,1:T(8,128)} %param.9) | copy-start | bytes 6148
  2.8 45.9 %all-to-all-start = ((f32[256,8,128]{2,1,0:T(8,128)}), f32[256,8,128]{2,1,0:T(8,128)S(1)}, u32[]{:S(2)}, u32[]{:S(2)}) async-start(f32[256,8,128]{2,1,0:T(8,128)} %bitcast.1), calls=%async_computation | async-start | bytes 2097152 | tf_op jit(solution)/shard_map/all_to_all | solution.py:312
  52.3 20.8 %all-to-all-start.1 = ((f32[16,16,8,128]{3,2,1,0:T(8,128)}), f32[16,16,8,128]{3,2,1,0:T(8,128)S(1)}, u32[]{:S(2)}, u32[]{:S(2)}) async-start(f32[16,16,8,128]{3,2,1,0:T(8,128)} %transform.1), calls=%async_computation.1 | async-start | bytes 2097152 | tf_op jit(solution)/shard_map/all_to_all | solution.py:315

commit v5 on v4

--- a/solution.py
+++ b/solution.py
@@ -89,6 +89,7 @@
     key = row * box_count + lane - lax.axis_index("sub") * per_peer
     place = jnp.zeros(place_ref.shape, jnp.int32)
     half = sub_count // 2
+    cases = coef_hbm.shape[1] // 8
     counts = [jnp.int32(0), jnp.int32(0)]
     ranks = []
     slots.wait()
@@ -102,12 +103,14 @@
         word = word + (jnp.int32(1) << shift_by)
         counts = [jnp.where(second, counts[0], word), jnp.where(second, word, counts[1])]
         place = jnp.where(key == peer * box_count + rank, slot % box_count, place)
-        ranks.append(peer * per_peer + rank)
+        ranks.append((rank, peer))
     place_ref[...] = place
     for box in range(box_count):
         if box % cut == 0:
             arriving[box // cut].wait()
-        out_ref[ranks[box]] = held[box]
+        rank, peer = ranks[box]
+        for case in range(cases):
+            out_ref[rank * cases + case, peer] = held[box, 8 * case : 8 * case + 8, :]
 
 
 def stage_kernel(table_hbm, high_hbm, rest_hbm, turn_hbm, place_ref, table_ref, high_ref, rest_ref, turn_ref, moved):
@@ -129,8 +132,9 @@
     return jnp.take_along_axis(value, order, axis=0)
 
 
-def transform_kernel(blk_count, in_ref, table_ref, high_ref, rest_ref, out_ref, cycles, made, moved):
-    boxes = in_ref.shape[0] // blk_count
+def transform_kernel(blk_count, in_ref, table_ref, high_ref, rest_ref, place_ref, out_ref, cycles, made, moved):
+    del place_ref
+    boxes = in_ref.shape[1]
     degrees = L // blk_count
     group = 2
     vregs = HALF // 8
@@ -145,7 +149,7 @@
             for one in range(2 * group):
                 box, part = step * group + one // 2, one % 2
                 at = part * degrees + row
-                value = in_ref[box * blk_count + source, at : at + 1, :]
+                value = in_ref[source, box, at : at + 1, :]
                 wide = jnp.broadcast_to(value, (8, M))
                 for v in range(vregs):
                     term = wide * table[v]
@@ -182,9 +186,9 @@
                 start = one * J + at
                 real = spread(waves[start : start + 8, :K], order)
                 imag = spread(waves[start : start + 8, K:], order)
-                made[blk, step * group + one] = jnp.where(real_row, real, imag)
+                made[step * group + one, blk] = jnp.where(real_row, real, imag)
         part = pl.ds(step * group, group)
-        pltpu.make_async_copy(made.at[:, part], out_ref.at[:, part], moved).start()
+        pltpu.make_async_copy(made.at[part], out_ref.at[part], moved).start()
 
     steps = boxes // group
     legendre(0, 0)
@@ -205,7 +209,7 @@
         box = place_ref[me, arrival]
         source = arrival // per_peer
         rank = arrival % per_peer
-        waves = [in_ref[rank * cases + case, source] for case in range(cases)]
+        waves = [in_ref[source, rank * cases + case] for case in range(cases)]
         crossed = [jnp.where(even, pltpu.roll(w, 7, 0), pltpu.roll(w, 1, 0)) for w in waves]
         for child in range(8):
             octant = child_ref[box, child]
@@ -238,9 +242,10 @@
 def pack(owner_slot, coefficients, sub_count):
     box_count = coefficients.shape[0]
     shape = (box_count, coefficients.size // (box_count * M), M)
+    sent = (box_count // sub_count * coefficients.shape[1], sub_count, 8, M)
     return pl.pallas_call(
         lambda *refs: pack_kernel(sub_count, *refs),
-        out_shape=(pltpu.VMEM(shape, F32), jax.ShapeDtypeStruct((sub_count, box_count), jnp.int32)),
+        out_shape=(pltpu.VMEM(sent, F32), jax.ShapeDtypeStruct((sub_count, box_count), jnp.int32)),
         in_specs=[whole(pl.ANY)] * 2,
         out_specs=(whole(pltpu.VMEM), whole(pltpu.VMEM)),
         scratch_shapes=[
@@ -271,13 +276,13 @@
     )(*[far(table) for table in tables], places)
 
 
-def transform(arrived, table, high, rest, blk_count):
-    boxes = arrived.shape[0] // blk_count
-    made = (blk_count, boxes, 8, K)
+def transform(arrived, table, high, rest, places):
+    blk_count, boxes = arrived.shape[:2]
+    made = (boxes, blk_count, 8, K)
     return pl.pallas_call(
         lambda *refs: transform_kernel(blk_count, *refs),
         out_shape=jax.ShapeDtypeStruct(made, F32),
-        in_specs=[whole(pltpu.VMEM)] * 4,
+        in_specs=[whole(pltpu.VMEM)] * 4 + [whole(pl.ANY)],
         out_specs=whole(pl.ANY),
         scratch_shapes=[
             pltpu.VMEM((2, 2 * J, 2 * M), F32),
@@ -286,12 +291,12 @@
         ],
         compiler_params=limit(16),
         name="transform",
-    )(near(arrived), near(table), near(high), near(rest))
+    )(near(arrived), near(table), near(high), near(rest), places)
 
 
 def shift(places, child_list, rows, turns):
     sub_count, boxes = places.shape
-    cases = rows.shape[0] * sub_count // boxes
+    cases = rows.shape[1] * sub_count // boxes
     shape = (boxes, cases * 8, 8, K)
     return pl.pallas_call(
         lambda *refs: shift_kernel(boxes, sub_count, *refs),
@@ -309,11 +314,11 @@
     blk_count = lax.axis_size("blk")
 
     outgoing, places = pack(owner_slot, coefficients, lax.axis_size("sub"))
-    arrived = lax.all_to_all(outgoing.reshape(box_count * cases, 8, M), ("sub", "blk"), 0, 0, tiled=True)
+    arrived = lax.all_to_all(outgoing, "blk", 0, 0, tiled=True)
     table, high, rest, turns = stage(places, blk_count)
-    waves = transform(arrived, table, high, rest, blk_count)
-    rows = lax.all_to_all(waves, "blk", 0, 0, tiled=True)
     places = lax.psum(places, "sub")
+    waves = transform(arrived, table, high, rest, places)
+    rows = lax.all_to_all(waves.reshape(-1, 8, K), ("sub", "blk"), 0, 0, tiled=True).reshape(waves.shape)
     children = shift(places, child_list, rows, turns)
     return children.reshape(box_count, cases, 8, J // blk_count, 2, K)
 

time: 77.9 us -> 77.9 us (level)
  blocking collectives: 13.8 us -> 17.5 us
  starting transfers between devices: 20.6 us -> 17.7 us
  waiting for transfers between devices: 31 us -> 30.1 us
    psum x1, blocking collectives: 13.8 us -> 17.5 us  [body(): places = lax.psum(places, 'sub')]
    all_to_all x2, starting transfers between devices: 20.6 us -> 17.7 us  [the longest x1 10.8 us: body(): lax.all_to_all(waves.reshape(-1, 8, K), ('sub', 'blk'), 0, 0, tiled=True)]
    all_to_all x2, waiting for transfers between devices: 31 us -> 30.1 us  [the longest x1 30.1 us: body(): lax.all_to_all(waves.reshape(-1, 8, K), ('sub', 'blk'), 0, 0, tiled=True)]
  transfers between devices with their start and end apart: 2 -> 2, of which waited for: 2 -> 1; matrix products, arithmetic and copies ran while one was open for 0% -> 0% of each run, Pallas kernels for 2% -> 2%
where the time goes in v5:
time: 77.9 us; the launch traced here: 77.6 us
  waiting for transfers between devices  30.1 us (39%)
  starting transfers between devices  17.7 us (23%)
  blocking collectives  17.5 us (22%)
  Pallas kernels  12.2 us (16%)
    all_to_all x1, waiting for transfers between devices, body(): lax.all_to_all(waves.reshape(-1, 8, K), ('sub', 'blk'), 0, 0, tiled=True)  30.1 us
    psum x1, blocking collectives, body(): places = lax.psum(places, 'sub')  17.5 us
    all_to_all x1, starting transfers between devices, body(): lax.all_to_all(waves.reshape(-1, 8, K), ('sub', 'blk'), 0, 0, tiled=True)  10.8 us
    all_to_all x1, starting transfers between devices, body(): arrived = lax.all_to_all(outgoing, 'blk', 0, 0, tiled=True)  6.93 us
    pallas_call x1, Pallas kernels, shift(): pl.pallas_call(lambda *refs: shift_kernel(boxes, sub_count, *refs), out_s...  4.47 us
    pallas_call x1, Pallas kernels, transform(): pl.pallas_call(lambda *refs: transform_kernel(blk_count, *refs), out_shap...  3.66 us
    pallas_call x1, Pallas kernels, pack(): pl.pallas_call(lambda *refs: pack_kernel(sub_count, *refs), out_shape=(pl...  2.75 us
  transfers between devices with their start and end apart: 2, of which 1 were waited for; matrix products, arithmetic and copies ran while one was open for 0% of the time, Pallas kernels for 2%

profile of v5, /device:TPU:1, one launch (start us, length us, event | category | flops | bytes accessed | tf_op | source)
XLA Modules:
  0.0 77.6 jit_solution(6828811083486091854)
XLA Ops:
  0.0 0.0 copy-start
  0.0 2.7 %pack.1 = (f32[16,16,8,128]{3,2,1,0:T(8,128)}, s32[16,64]{1,0:T(8,128)S(1)}) custom-call(s32[64]{0:T(128)} %refs_0_.1, f32[64,32,128]{2,1,0:T(8,128)} %bitcast.5), custom_call_target="tpu_custom_call" | custom-call | tf_op jit(solution)/shard_map/pack/pallas_call | solution.py:246
  2.8 6.9 %all-to-all-start = ((f32[16,16,8,128]{3,2,1,0:T(8,128)}), f32[16,16,8,128]{3,2,1,0:T(8,128)S(1)}, u32[]{:S(2)}, u32[]{:S(2)}) async-start(f32[16,16,8,128]{3,2,1,0:T(8,128)} %get-tuple-element.12), calls=%async_computation | async-start | bytes 2097152 | tf_op jit(solution)/shard_map/all_to_all | solution.py:317
  9.7 1.3 %stage.1 = (f32[64,32,128]{2,1,0:T(8,128)S(1)}, bf16[256,256]{1,0:T(8,128)(2,1)S(1)}, bf16[256,256]{1,0:T(8,128)(2,1)S(1)}, f32[8,2,8,128]{3,2,1,0:T(8,128)S(1)}) custom-call(f32[64,32,128]{2,1,0:T(8,128)} %constant.8.clone.table_hbm, bf16[256,256]{1,0:T(8,128)(2,1)} %constant.9.clone.high_hbm, bf16[256,256]{1,0:T(8,128)(2,1)} %constant.10.clone.rest_hbm, ...), custom_call_target="tpu_custom_call" | custom-call | bytes 4194304 | tf_op jit(solution)/shard_map/stage/pallas_call | solution.py:267
  11.0 17.5 %psum.7.refs_4_.refs_0_ = s32[16,64]{1,0:T(8,128)S(1)} all-reduce(s32[16,64]{1,0:T(8,128)S(1)} %get-tuple-element.11.place_ref), channel_id=1, replica_groups=mesh['sub'=16,'blk'=16] {'sub'}, use_global_device_ids=true, to_apply=%region_0.0 | all-reduce | flops 1024 | bytes 8192 | tf_op jit(solution)/shard_map/psum | solution.py:319
  28.5 0.0 all-to-all-done.refs_0_
  28.5 3.7 %transform.1 = f32[16,16,8,128]{3,2,1,0:T(8,128)} custom-call(f32[16,16,8,128]{3,2,1,0:T(8,128)S(1)} %all-to-all-done.refs_0_, f32[64,32,128]{2,1,0:T(8,128)S(1)} %get-tuple-element.13.refs_1_, bf16[256,256]{1,0:T(8,128)(2,1)S(1)} %get-tuple-element.14.refs_2_, bf16[256,256]{1,0:T(8,128)(2,1)S(1)} %get-tuple-element.15.refs_3_, s32[16,64]{1,0:T(8,128)S(1)} %psum.7.refs_4_.refs_0_), custom_call_target="tpu_custom_call" | custom-call | tf_op jit(solution)/shard_map/transform/pallas_call | solution.py:282
  32.2 10.8 %all-to-all-start.1 = ((f32[256,8,128]{2,1,0:T(8,128)}), f32[256,8,128]{2,1,0:T(8,128)S(1)}, u32[]{:S(2)}, u32[]{:S(2)}) async-start(f32[256,8,128]{2,1,0:T(8,128)} %bitcast.1), calls=%async_computation.1 | async-start | bytes 2097152 | tf_op jit(solution)/shard_map/all_to_all | solution.py:321
  42.9 0.0 copy-done
  43.0 0.1 copy.8.refs_1_
  43.0 30.1 %all-to-all-done.1 = f32[256,8,128]{2,1,0:T(8,128)S(1)} async-done(((f32[256,8,128]{2,1,0:T(8,128)}), f32[256,8,128]{2,1,0:T(8,128)S(1)}, u32[]{:S(2)}, u32[]{:S(2)}) %all-to-all-start.1) | async-done | bytes 1048608 | tf_op jit(solution)/shard_map/all_to_all | solution.py:321
  73.2 4.5 %shift.1 = f32[64,32,8,128]{3,2,1,0:T(8,128)} custom-call(s32[16,64]{1,0:T(8,128)S(1)} %psum.7.refs_4_.refs_0_, s32[64,8]{1,0:T(8,128)S(1)} %copy.8.refs_1_, f32[16,16,8,128]{3,2,1,0:T(8,128)S(1)} %bitcast.4, f32[8,2,8,128]{3,2,1,0:T(8,128)S(1)} %get-tuple-element.16.refs_3_), custom_call_target="tpu_custom_call" | custom-call | tf_op jit(solution)/shard_map/shift/pallas_call | solution.py:301
Async XLA Ops:
  0.0 42.9 %copy-start = (s32[64,8]{0,1:T(8,128)S(1)}, s32[64,8]{0,1:T(8,128)}, u32[]{:S(2)}) copy-start(s32[64,8]{0,1:T(8,128)} %param.9) | copy-start | bytes 6148
  2.8 25.8 %all-to-all-start = ((f32[16,16,8,128]{3,2,1,0:T(8,128)}), f32[16,16,8,128]{3,2,1,0:T(8,128)S(1)}, u32[]{:S(2)}, u32[]{:S(2)}) async-start(f32[16,16,8,128]{3,2,1,0:T(8,128)} %get-tuple-element.12), calls=%async_computation | async-start | bytes 2097152 | tf_op jit(solution)/shard_map/all_to_all | solution.py:317
  32.2 41.0 %all-to-all-start.1 = ((f32[256,8,128]{2,1,0:T(8,128)}), f32[256,8,128]{2,1,0:T(8,128)S(1)}, u32[]{:S(2)}, u32[]{:S(2)}) async-start(f32[256,8,128]{2,1,0:T(8,128)} %bitcast.1), calls=%async_computation.1 | async-start | bytes 2097152 | tf_op jit(solution)/shard_map/all_to_all | solution.py:321

commit v6 on v5

--- a/solution.py
+++ b/solution.py
@@ -71,7 +71,10 @@
     return cut(cosine), cut(sine)
 
 
-def pack_kernel(sub_count, slot_hbm, coef_hbm, out_ref, place_ref, slot_ref, held, slot_in, coef_in):
+def pack_kernel(sub_count, slot_hbm, coef_hbm, *refs):
+    tables, refs = refs[:4], refs[4:]
+    out_ref, place_ref, *staged = refs[:6]
+    slot_ref, held, slot_in, coef_in, table_in = refs[6:]
     box_count = coef_hbm.shape[0]
     per_peer = box_count // sub_count
     pieces = coef_in.shape[0]
@@ -84,9 +87,13 @@
         arriving.append(pltpu.make_async_copy(coef_hbm.at[part], held.at[part], coef_in.at[piece]))
     for copy in arriving:
         copy.start()
+    tables = tables[:3] + (tables[3].at[lax.axis_index("blk")],)
+    staging = [pltpu.make_async_copy(a, b, table_in.at[at]) for at, (a, b) in enumerate(zip(tables, staged))]
+    for copy in staging:
+        copy.start()
     row = lax.broadcasted_iota(jnp.int32, place_ref.shape, 0)
     lane = lax.broadcasted_iota(jnp.int32, place_ref.shape, 1)
-    key = row * box_count + lane - lax.axis_index("sub") * per_peer
+    key = row * place_ref.shape[1] + lane - lax.axis_index("sub") * per_peer
     place = jnp.zeros(place_ref.shape, jnp.int32)
     half = sub_count // 2
     cases = coef_hbm.shape[1] // 8
@@ -111,20 +118,7 @@
         rank, peer = ranks[box]
         for case in range(cases):
             out_ref[rank * cases + case, peer] = held[box, 8 * case : 8 * case + 8, :]
-
-
-def stage_kernel(table_hbm, high_hbm, rest_hbm, turn_hbm, place_ref, table_ref, high_ref, rest_ref, turn_ref, moved):
-    del place_ref
-    pairs = [
-        (table_hbm, table_ref),
-        (high_hbm, high_ref),
-        (rest_hbm, rest_ref),
-        (turn_hbm.at[lax.axis_index("blk")], turn_ref),
-    ]
-    copies = [pltpu.make_async_copy(source, target, moved.at[at]) for at, (source, target) in enumerate(pairs)]
-    for copy in copies:
-        copy.start()
-    for copy in copies:
+    for copy in staging:
         copy.wait()
 
 
@@ -206,7 +200,8 @@
     me = lax.axis_index("sub")
 
     def one_box(arrival, carry):
-        box = place_ref[me, arrival]
+        at = me * boxes + arrival
+        box = place_ref[at // 128, at % 128]
         source = arrival // per_peer
         rank = arrival % per_peer
         waves = [in_ref[source, rank * cases + case] for case in range(cases)]
@@ -239,41 +234,30 @@
     return pltpu.with_memory_space_constraint(array, pltpu.HBM)
 
 
-def pack(owner_slot, coefficients, sub_count):
+def pack(owner_slot, coefficients, sub_count, blk_count):
+    high, rest = dft_halves()
+    tables = [legendre_half(), high, rest, np.stack(shift_tables(blk_count), axis=2)]
+    tables = [jnp.asarray(table) for table in tables]
+    shapes = [table.shape for table in tables[:3]] + [tables[3].shape[1:]]
     box_count = coefficients.shape[0]
     shape = (box_count, coefficients.size // (box_count * M), M)
     sent = (box_count // sub_count * coefficients.shape[1], sub_count, 8, M)
     return pl.pallas_call(
         lambda *refs: pack_kernel(sub_count, *refs),
-        out_shape=(pltpu.VMEM(sent, F32), jax.ShapeDtypeStruct((sub_count, box_count), jnp.int32)),
-        in_specs=[whole(pl.ANY)] * 2,
-        out_specs=(whole(pltpu.VMEM), whole(pltpu.VMEM)),
+        out_shape=(pltpu.VMEM(sent, F32), jax.ShapeDtypeStruct((sub_count * box_count // 128, 128), jnp.int32))
+        + tuple(pltpu.VMEM(shape, table.dtype) for shape, table in zip(shapes, tables)),
+        in_specs=[whole(pl.ANY)] * 6,
+        out_specs=(whole(pltpu.VMEM),) * 6,
         scratch_shapes=[
             pltpu.SMEM((box_count,), jnp.int32),
             pltpu.VMEM(shape, F32),
             pltpu.SemaphoreType.DMA,
             pltpu.SemaphoreType.DMA((4,)),
+            pltpu.SemaphoreType.DMA((4,)),
         ],
         compiler_params=limit(16),
         name="pack",
-    )(far(owner_slot), far(coefficients.reshape(shape)))
-
-
-def stage(places, blk_count):
-    high, rest = dft_halves()
-    tables = [legendre_half(), high, rest, np.stack(shift_tables(blk_count), axis=2)]
-    tables = [jnp.asarray(table) for table in tables]
-    shapes = [table.shape for table in tables[:3]] + [tables[3].shape[1:]]
-    return pl.pallas_call(
-        stage_kernel,
-        out_shape=[pltpu.VMEM(shape, table.dtype) for shape, table in zip(shapes, tables)],
-        in_specs=[whole(pl.ANY)] * 5,
-        out_specs=[whole(pltpu.VMEM)] * 4,
-        scratch_shapes=[pltpu.SemaphoreType.DMA((4,))],
-        compiler_params=limit(4),
-        cost_estimate=pl.CostEstimate(flops=0, bytes_accessed=4 * 2**20, transcendentals=0),
-        name="stage",
-    )(*[far(table) for table in tables], places)
+    )(far(owner_slot), far(coefficients.reshape(shape)), *[far(table) for table in tables])
 
 
 def transform(arrived, table, high, rest, places):
@@ -295,7 +279,7 @@
 
 
 def shift(places, child_list, rows, turns):
-    sub_count, boxes = places.shape
+    boxes, sub_count = child_list.shape[0], rows.shape[0]
     cases = rows.shape[1] * sub_count // boxes
     shape = (boxes, cases * 8, 8, K)
     return pl.pallas_call(
@@ -313,9 +297,8 @@
     box_count, cases = coefficients.shape[:2]
     blk_count = lax.axis_size("blk")
 
-    outgoing, places = pack(owner_slot, coefficients, lax.axis_size("sub"))
+    outgoing, places, table, high, rest, turns = pack(owner_slot, coefficients, lax.axis_size("sub"), blk_count)
     arrived = lax.all_to_all(outgoing, "blk", 0, 0, tiled=True)
-    table, high, rest, turns = stage(places, blk_count)
     places = lax.psum(places, "sub")
     waves = transform(arrived, table, high, rest, places)
     rows = lax.all_to_all(waves.reshape(-1, 8, K), ("sub", "blk"), 0, 0, tiled=True).reshape(waves.shape)

time: 77.9 us -> 77.1 us (0.990)
  Pallas kernels: 12.2 us -> 10.8 us
    pallas_call x1 -> x0, Pallas kernels: 1.29 us -> none  [stage(): pl.pallas_call(stage_kernel, out_shape=[pltpu.VMEM(shape, table.dtype) fo...]
  transfers between devices with their start and end apart: 2 -> 2, of which waited for: 1 -> 1; matrix products, arithmetic and copies ran while one was open for 0% -> 0% of each run, Pallas kernels for 2% -> 0%
where the time goes in v6:
time: 77.1 us; the launch traced here: 76.8 us
  waiting for transfers between devices  30.1 us (39%)
  starting transfers between devices  18.4 us (24%)
  blocking collectives  17.3 us (22%)
  Pallas kernels  10.8 us (14%)
    all_to_all x1, waiting for transfers between devices, body(): lax.all_to_all(waves.reshape(-1, 8, K), ('sub', 'blk'), 0, 0, tiled=True)  30.1 us
    psum x1, blocking collectives, body(): places = lax.psum(places, 'sub')  17.3 us
    all_to_all x1, starting transfers between devices, body(): lax.all_to_all(waves.reshape(-1, 8, K), ('sub', 'blk'), 0, 0, tiled=True)  11.5 us
    all_to_all x1, starting transfers between devices, body(): arrived = lax.all_to_all(outgoing, 'blk', 0, 0, tiled=True)  6.93 us
    pallas_call x1, Pallas kernels, shift(): pl.pallas_call(lambda *refs: shift_kernel(boxes, sub_count, *refs), out_s...  4.41 us
    pallas_call x1, Pallas kernels, transform(): pl.pallas_call(lambda *refs: transform_kernel(blk_count, *refs), out_shap...  3.66 us
    pallas_call x1, Pallas kernels, pack(): pl.pallas_call(lambda *refs: pack_kernel(sub_count, *refs), out_shape=(pl...  2.75 us
  transfers between devices with their start and end apart: 2, of which 1 were waited for; matrix products, arithmetic and copies ran while one was open for 0% of the time, Pallas kernels for 0%

profile of v6, /device:TPU:1, one launch (start us, length us, event | category | flops | bytes accessed | tf_op | source)
XLA Modules:
  0.0 76.8 jit_solution(10682844169794202084)
XLA Ops:
  0.0 0.0 copy-start
  0.0 2.8 %pack.1 = (f32[16,16,8,128]{3,2,1,0:T(8,128)}, s32[8,128]{1,0:T(8,128)S(1)}, f32[64,32,128]{2,1,0:T(8,128)S(1)}, bf16[256,256]{1,0:T(8,128)(2,1)S(1)}, bf16[256,...) custom-call(s32[64]{0:T(128)} %refs_0_.1, f32[64,32,128]{2,1,0:T(8,128)} %bitcast.5, ...), custom_call_target="tpu_custom_call" | custom-call | tf_op jit(solution)/shard_map/pack/pallas_call | solution.py:245
  2.8 6.9 %all-to-all-start = ((f32[16,16,8,128]{3,2,1,0:T(8,128)}), f32[16,16,8,128]{3,2,1,0:T(8,128)S(1)}, u32[]{:S(2)}, u32[]{:S(2)}) async-start(f32[16,16,8,128]{3,2,1,0:T(8,128)} %get-tuple-element.12), calls=%async_computation | async-start | bytes 2097152 | tf_op jit(solution)/shard_map/all_to_all | solution.py:301
  9.7 17.3 %psum.7.refs_4_.refs_0_ = s32[8,128]{1,0:T(8,128)S(1)} all-reduce(s32[8,128]{1,0:T(8,128)S(1)} %get-tuple-element.11), channel_id=1, replica_groups=mesh['sub'=16,'blk'=16] {'sub'}, use_global_device_ids=true, to_apply=%region_0.0 | all-reduce | flops 1024 | bytes 8192 | tf_op jit(solution)/shard_map/psum | solution.py:302
  27.0 0.0 all-to-all-done.refs_0_
  27.0 3.7 %transform.1 = f32[16,16,8,128]{3,2,1,0:T(8,128)} custom-call(f32[16,16,8,128]{3,2,1,0:T(8,128)S(1)} %all-to-all-done.refs_0_, f32[64,32,128]{2,1,0:T(8,128)S(1)} %get-tuple-element.13.refs_1_, bf16[256,256]{1,0:T(8,128)(2,1)S(1)} %get-tuple-element.14.refs_2_, bf16[256,256]{1,0:T(8,128)(2,1)S(1)} %get-tuple-element.15.refs_3_, s32[8,128]{1,0:T(8,128)S(1)} %psum.7.refs_4_.refs_0_), custom_call_target="tpu_custom_call" | custom-call | tf_op jit(solution)/shard_map/transform/pallas_call | solution.py:266
  30.7 11.5 %all-to-all-start.1 = ((f32[256,8,128]{2,1,0:T(8,128)}), f32[256,8,128]{2,1,0:T(8,128)S(1)}, u32[]{:S(2)}, u32[]{:S(2)}) async-start(f32[256,8,128]{2,1,0:T(8,128)} %bitcast.1), calls=%async_computation.1 | async-start | bytes 2097152 | tf_op jit(solution)/shard_map/all_to_all | solution.py:304
  42.2 0.0 copy-done
  42.2 0.1 copy.8.refs_1_
  42.3 30.1 %all-to-all-done.1 = f32[256,8,128]{2,1,0:T(8,128)S(1)} async-done(((f32[256,8,128]{2,1,0:T(8,128)}), f32[256,8,128]{2,1,0:T(8,128)S(1)}, u32[]{:S(2)}, u32[]{:S(2)}) %all-to-all-start.1) | async-done | bytes 1048608 | tf_op jit(solution)/shard_map/all_to_all | solution.py:304
  72.4 4.4 %shift.1 = f32[64,32,8,128]{3,2,1,0:T(8,128)} custom-call(s32[8,128]{1,0:T(8,128)S(1)} %psum.7.refs_4_.refs_0_, s32[64,8]{1,0:T(8,128)S(1)} %copy.8.refs_1_, f32[16,16,8,128]{3,2,1,0:T(8,128)S(1)} %bitcast.4, f32[8,2,8,128]{3,2,1,0:T(8,128)S(1)} %get-tuple-element.16.refs_3_), custom_call_target="tpu_custom_call" | custom-call | tf_op jit(solution)/shard_map/shift/pallas_call | solution.py:285
Async XLA Ops:
  0.0 42.2 %copy-start = (s32[64,8]{0,1:T(8,128)S(1)}, s32[64,8]{0,1:T(8,128)}, u32[]{:S(2)}) copy-start(s32[64,8]{0,1:T(8,128)} %param.9) | copy-start | bytes 6148
  2.8 24.2 %all-to-all-start = ((f32[16,16,8,128]{3,2,1,0:T(8,128)}), f32[16,16,8,128]{3,2,1,0:T(8,128)S(1)}, u32[]{:S(2)}, u32[]{:S(2)}) async-start(f32[16,16,8,128]{3,2,1,0:T(8,128)} %get-tuple-element.12), calls=%async_computation | async-start | bytes 2097152 | tf_op jit(solution)/shard_map/all_to_all | solution.py:301
  30.7 41.7 %all-to-all-start.1 = ((f32[256,8,128]{2,1,0:T(8,128)}), f32[256,8,128]{2,1,0:T(8,128)S(1)}, u32[]{:S(2)}, u32[]{:S(2)}) async-start(f32[256,8,128]{2,1,0:T(8,128)} %bitcast.1), calls=%async_computation.1 | async-start | bytes 2097152 | tf_op jit(solution)/shard_map/all_to_all | solution.py:304

commit v7 on v6

--- a/solution.py
+++ b/solution.py
@@ -77,6 +77,7 @@
     slot_ref, held, slot_in, coef_in, table_in = refs[6:]
     box_count = coef_hbm.shape[0]
     per_peer = box_count // sub_count
+    box_bits = box_count.bit_length() - 1
     pieces = coef_in.shape[0]
     cut = box_count // pieces
     slots = pltpu.make_async_copy(slot_hbm, slot_ref, slot_in)
@@ -102,14 +103,14 @@
     slots.wait()
     for box in range(box_count):
         slot = slot_ref[box]
-        peer = slot // box_count
+        peer = slot >> box_bits
         second = peer >= half
-        shift_by = (peer % half) * 4
+        shift_by = (peer & (half - 1)) << 2
         word = jnp.where(second, counts[1], counts[0])
         rank = (word >> shift_by) & 7
         word = word + (jnp.int32(1) << shift_by)
         counts = [jnp.where(second, counts[0], word), jnp.where(second, word, counts[1])]
-        place = jnp.where(key == peer * box_count + rank, slot % box_count, place)
+        place = jnp.where(key == (peer << box_bits) + rank, slot & (box_count - 1), place)
         ranks.append((rank, peer))
     place_ref[...] = place
     for box in range(box_count):
@@ -201,13 +202,14 @@
 
     def one_box(arrival, carry):
         at = me * boxes + arrival
-        box = place_ref[at // 128, at % 128]
+        box = place_ref[at >> 7, at & 127]
         source = arrival // per_peer
         rank = arrival % per_peer
+        row, first = box >> 4, (box & 15) * 8
         waves = [in_ref[source, rank * cases + case] for case in range(cases)]
         crossed = [jnp.where(even, pltpu.roll(w, 7, 0), pltpu.roll(w, 1, 0)) for w in waves]
         for child in range(8):
-            octant = child_ref[box, child]
+            octant = child_ref[row, first + child]
             cosine, sine = turn_ref[octant, 0], turn_ref[octant, 1]
             for case in range(cases):
                 made[arrival, case * 8 + child] = waves[case] * cosine + crossed[case] * sine
@@ -280,6 +282,7 @@
 
 def shift(places, child_list, rows, turns):
     boxes, sub_count = child_list.shape[0], rows.shape[0]
+    child_list = child_list.reshape(-1, 128)
     cases = rows.shape[1] * sub_count // boxes
     shape = (boxes, cases * 8, 8, K)
     return pl.pallas_call(

time: 77.1 us -> 76.5 us (level)
  no operation moved by 1% of the time
where the time goes in v7:
time: 76.5 us; the launch traced here: 76.2 us
  waiting for transfers between devices  30 us (39%)
  starting transfers between devices  18.4 us (24%)
  blocking collectives  17.3 us (23%)
  Pallas kernels  10.2 us (13%)
    all_to_all x1, waiting for transfers between devices, body(): lax.all_to_all(waves.reshape(-1, 8, K), ('sub', 'blk'), 0, 0, tiled=True)  30 us
    psum x1, blocking collectives, body(): places = lax.psum(places, 'sub')  17.3 us
    all_to_all x1, starting transfers between devices, body(): lax.all_to_all(waves.reshape(-1, 8, K), ('sub', 'blk'), 0, 0, tiled=True)  11.5 us
    all_to_all x1, starting transfers between devices, body(): arrived = lax.all_to_all(outgoing, 'blk', 0, 0, tiled=True)  6.93 us
    pallas_call x1, Pallas kernels, shift(): pl.pallas_call(lambda *refs: shift_kernel(boxes, sub_count, *refs), out_s...  3.91 us
    pallas_call x1, Pallas kernels, transform(): pl.pallas_call(lambda *refs: transform_kernel(blk_count, *refs), out_shap...  3.66 us
    pallas_call x1, Pallas kernels, pack(): pl.pallas_call(lambda *refs: pack_kernel(sub_count, *refs), out_shape=(pl...  2.67 us
  transfers between devices with their start and end apart: 2, of which 1 were waited for; matrix products, arithmetic and copies ran while one was open for 0% of the time, Pallas kernels for 0%

profile of v7, /device:TPU:1, one launch (start us, length us, event | category | flops | bytes accessed | tf_op | source)
XLA Modules:
  0.0 76.2 jit_solution(15290326420583413209)
XLA Ops:
  0.0 0.0 copy-start
  0.0 2.7 %pack.1 = (f32[16,16,8,128]{3,2,1,0:T(8,128)}, s32[8,128]{1,0:T(8,128)S(1)}, f32[64,32,128]{2,1,0:T(8,128)S(1)}, bf16[256,256]{1,0:T(8,128)(2,1)S(1)}, bf16[256,...) custom-call(s32[64]{0:T(128)} %refs_0_.1, f32[64,32,128]{2,1,0:T(8,128)} %bitcast.5, ...), custom_call_target="tpu_custom_call" | custom-call | tf_op jit(solution)/shard_map/pack/pallas_call | solution.py:247
  2.7 6.9 %all-to-all-start = ((f32[16,16,8,128]{3,2,1,0:T(8,128)}), f32[16,16,8,128]{3,2,1,0:T(8,128)S(1)}, u32[]{:S(2)}, u32[]{:S(2)}) async-start(f32[16,16,8,128]{3,2,1,0:T(8,128)} %get-tuple-element.12), calls=%async_computation | async-start | bytes 2097152 | tf_op jit(solution)/shard_map/all_to_all | solution.py:304
  9.6 17.3 %psum.7.refs_4_.refs_0_ = s32[8,128]{1,0:T(8,128)S(1)} all-reduce(s32[8,128]{1,0:T(8,128)S(1)} %get-tuple-element.11), channel_id=1, replica_groups=mesh['sub'=16,'blk'=16] {'sub'}, use_global_device_ids=true, to_apply=%region_0.0 | all-reduce | flops 1024 | bytes 8192 | tf_op jit(solution)/shard_map/psum | solution.py:305
  26.9 0.0 all-to-all-done.refs_0_
  26.9 3.7 %transform.1 = f32[16,16,8,128]{3,2,1,0:T(8,128)} custom-call(f32[16,16,8,128]{3,2,1,0:T(8,128)S(1)} %all-to-all-done.refs_0_, f32[64,32,128]{2,1,0:T(8,128)S(1)} %get-tuple-element.13.refs_1_, bf16[256,256]{1,0:T(8,128)(2,1)S(1)} %get-tuple-element.14.refs_2_, bf16[256,256]{1,0:T(8,128)(2,1)S(1)} %get-tuple-element.15.refs_3_, s32[8,128]{1,0:T(8,128)S(1)} %psum.7.refs_4_.refs_0_), custom_call_target="tpu_custom_call" | custom-call | tf_op jit(solution)/shard_map/transform/pallas_call | solution.py:268
  30.6 11.5 %all-to-all-start.1 = ((f32[256,8,128]{2,1,0:T(8,128)}), f32[256,8,128]{2,1,0:T(8,128)S(1)}, u32[]{:S(2)}, u32[]{:S(2)}) async-start(f32[256,8,128]{2,1,0:T(8,128)} %bitcast.1), calls=%async_computation.1 | async-start | bytes 2097152 | tf_op jit(solution)/shard_map/all_to_all | solution.py:307
  42.1 0.0 copy-done
  42.1 0.1 copy.9
  42.2 0.1 reshape.16.refs_1_
  42.3 30.0 %all-to-all-done.1 = f32[256,8,128]{2,1,0:T(8,128)S(1)} async-done(((f32[256,8,128]{2,1,0:T(8,128)}), f32[256,8,128]{2,1,0:T(8,128)S(1)}, u32[]{:S(2)}, u32[]{:S(2)}) %all-to-all-start.1) | async-done | bytes 1048608 | tf_op jit(solution)/shard_map/all_to_all | solution.py:307
  72.3 3.9 %shift.1 = f32[64,32,8,128]{3,2,1,0:T(8,128)} custom-call(s32[8,128]{1,0:T(8,128)S(1)} %psum.7.refs_4_.refs_0_, s32[4,128]{1,0:T(4,128)S(1)} %reshape.16.refs_1_, f32[16,16,8,128]{3,2,1,0:T(8,128)S(1)} %bitcast.4, f32[8,2,8,128]{3,2,1,0:T(8,128)S(1)} %get-tuple-element.16.refs_3_), custom_call_target="tpu_custom_call" | custom-call | tf_op jit(solution)/shard_map/shift/pallas_call | solution.py:288
Async XLA Ops:
  0.0 42.1 %copy-start = (s32[64,8]{0,1:T(8,128)S(1)}, s32[64,8]{0,1:T(8,128)}, u32[]{:S(2)}) copy-start(s32[64,8]{0,1:T(8,128)} %param.9) | copy-start | bytes 6148
  2.7 24.2 %all-to-all-start = ((f32[16,16,8,128]{3,2,1,0:T(8,128)}), f32[16,16,8,128]{3,2,1,0:T(8,128)S(1)}, u32[]{:S(2)}, u32[]{:S(2)}) async-start(f32[16,16,8,128]{3,2,1,0:T(8,128)} %get-tuple-element.12), calls=%async_computation | async-start | bytes 2097152 | tf_op jit(solution)/shard_map/all_to_all | solution.py:304
  30.6 41.7 %all-to-all-start.1 = ((f32[256,8,128]{2,1,0:T(8,128)}), f32[256,8,128]{2,1,0:T(8,128)S(1)}, u32[]{:S(2)}, u32[]{:S(2)}) async-start(f32[256,8,128]{2,1,0:T(8,128)} %bitcast.1), calls=%async_computation.1 | async-start | bytes 2097152 | tf_op jit(solution)/shard_map/all_to_all | solution.py:307

commit v8 on v7

--- a/solution.py
+++ b/solution.py
@@ -131,18 +131,17 @@
     del place_ref
     boxes = in_ref.shape[1]
     degrees = L // blk_count
-    group = 2
     vregs = HALF // 8
     lane = lax.broadcasted_iota(jnp.int32, (8, M), 1)
     mirror = jnp.where(lane % 2 == 0, 1.0, -1.0).astype(F32)
 
-    def legendre(step, slot):
+    def legendre(start_box, group, slot):
         sums = [[[None] * vregs for _ in range(2)] for _ in range(2 * group)]
         for degree in range(L):
             source, row = degree // degrees, degree % degrees
             table = [table_ref[degree, 8 * v : 8 * v + 8, :] for v in range(vregs)]
             for one in range(2 * group):
-                box, part = step * group + one // 2, one % 2
+                box, part = start_box + one // 2, one % 2
                 at = part * degrees + row
                 value = in_ref[source, box, at : at + 1, :]
                 wide = jnp.broadcast_to(value, (8, M))
@@ -163,8 +162,8 @@
     real_row = sub_row % 2 == 0
     step_row = sub_row // 2
 
-    def azimuths(step, slot):
-        left = cycles[slot]
+    def azimuths(start_box, group, slot):
+        left = cycles[slot, : group * J]
         left_high = left.astype(BF16)
         left_rest = (left - left_high.astype(F32)).astype(BF16)
         waves = jnp.dot(left_high, high_ref[...], preferred_element_type=F32)
@@ -181,16 +180,17 @@
                 start = one * J + at
                 real = spread(waves[start : start + 8, :K], order)
                 imag = spread(waves[start : start + 8, K:], order)
-                made[step * group + one, blk] = jnp.where(real_row, real, imag)
-        part = pl.ds(step * group, group)
+                made[start_box + one, blk] = jnp.where(real_row, real, imag)
+        part = pl.ds(start_box, group)
         pltpu.make_async_copy(made.at[part], out_ref.at[part], moved).start()
 
-    steps = boxes // group
-    legendre(0, 0)
-    for step in range(1, steps):
-        azimuths(step - 1, (step - 1) % 2)
-        legendre(step, step % 2)
-    azimuths(steps - 1, (steps - 1) % 2)
+    sizes = [1] * boxes
+    starts = [sum(sizes[:step]) for step in range(len(sizes))]
+    legendre(starts[0], sizes[0], 0)
+    for step in range(1, len(sizes)):
+        azimuths(starts[step - 1], sizes[step - 1], (step - 1) % 2)
+        legendre(starts[step], sizes[step], step % 2)
+    azimuths(starts[-1], sizes[-1], (len(sizes) - 1) % 2)
     pltpu.make_async_copy(made, out_ref, moved).wait()
 
 

time: 76.5 us -> 76.5 us (level)
  no operation moved by 1% of the time
where the time goes in v8:
time: 76.5 us; the launch traced here: 76.2 us
  waiting for transfers between devices  30 us (39%)
  starting transfers between devices  18.4 us (24%)
  blocking collectives  17.3 us (23%)
  Pallas kernels  10.2 us (13%)
    all_to_all x1, waiting for transfers between devices, body(): lax.all_to_all(waves.reshape(-1, 8, K), ('sub', 'blk'), 0, 0, tiled=True)  30 us
    psum x1, blocking collectives, body(): places = lax.psum(places, 'sub')  17.3 us
    all_to_all x1, starting transfers between devices, body(): lax.all_to_all(waves.reshape(-1, 8, K), ('sub', 'blk'), 0, 0, tiled=True)  11.5 us
    all_to_all x1, starting transfers between devices, body(): arrived = lax.all_to_all(outgoing, 'blk', 0, 0, tiled=True)  6.93 us
    pallas_call x1, Pallas kernels, shift(): pl.pallas_call(lambda *refs: shift_kernel(boxes, sub_count, *refs), out_s...  3.91 us
    pallas_call x1, Pallas kernels, transform(): pl.pallas_call(lambda *refs: transform_kernel(blk_count, *refs), out_shap...  3.62 us
    pallas_call x1, Pallas kernels, pack(): pl.pallas_call(lambda *refs: pack_kernel(sub_count, *refs), out_shape=(pl...  2.67 us
  transfers between devices with their start and end apart: 2, of which 1 were waited for; matrix products, arithmetic and copies ran while one was open for 0% of the time, Pallas kernels for 0%

profile of v8, /device:TPU:1, one launch (start us, length us, event | category | flops | bytes accessed | tf_op | source)
XLA Modules:
  0.0 76.2 jit_solution(6895643752112211501)
XLA Ops:
  0.0 0.0 copy-start
  0.0 2.7 %pack.1 = (f32[16,16,8,128]{3,2,1,0:T(8,128)}, s32[8,128]{1,0:T(8,128)S(1)}, f32[64,32,128]{2,1,0:T(8,128)S(1)}, bf16[256,256]{1,0:T(8,128)(2,1)S(1)}, bf16[256,...) custom-call(s32[64]{0:T(128)} %refs_0_.1, f32[64,32,128]{2,1,0:T(8,128)} %bitcast.5, ...), custom_call_target="tpu_custom_call" | custom-call | tf_op jit(solution)/shard_map/pack/pallas_call | solution.py:247
  2.7 6.9 %all-to-all-start = ((f32[16,16,8,128]{3,2,1,0:T(8,128)}), f32[16,16,8,128]{3,2,1,0:T(8,128)S(1)}, u32[]{:S(2)}, u32[]{:S(2)}) async-start(f32[16,16,8,128]{3,2,1,0:T(8,128)} %get-tuple-element.12), calls=%async_computation | async-start | bytes 2097152 | tf_op jit(solution)/shard_map/all_to_all | solution.py:304
  9.6 17.3 %psum.7.refs_4_.refs_0_ = s32[8,128]{1,0:T(8,128)S(1)} all-reduce(s32[8,128]{1,0:T(8,128)S(1)} %get-tuple-element.11), channel_id=1, replica_groups=mesh['sub'=16,'blk'=16] {'sub'}, use_global_device_ids=true, to_apply=%region_0.0 | all-reduce | flops 1024 | bytes 8192 | tf_op jit(solution)/shard_map/psum | solution.py:305
  26.9 0.0 all-to-all-done.refs_0_
  26.9 3.6 %transform.1 = f32[16,16,8,128]{3,2,1,0:T(8,128)} custom-call(f32[16,16,8,128]{3,2,1,0:T(8,128)S(1)} %all-to-all-done.refs_0_, f32[64,32,128]{2,1,0:T(8,128)S(1)} %get-tuple-element.13.refs_1_, bf16[256,256]{1,0:T(8,128)(2,1)S(1)} %get-tuple-element.14.refs_2_, bf16[256,256]{1,0:T(8,128)(2,1)S(1)} %get-tuple-element.15.refs_3_, s32[8,128]{1,0:T(8,128)S(1)} %psum.7.refs_4_.refs_0_), custom_call_target="tpu_custom_call" | custom-call | tf_op jit(solution)/shard_map/transform/pallas_call | solution.py:268
  30.5 11.5 %all-to-all-start.1 = ((f32[256,8,128]{2,1,0:T(8,128)}), f32[256,8,128]{2,1,0:T(8,128)S(1)}, u32[]{:S(2)}, u32[]{:S(2)}) async-start(f32[256,8,128]{2,1,0:T(8,128)} %bitcast.1), calls=%async_computation.1 | async-start | bytes 2097152 | tf_op jit(solution)/shard_map/all_to_all | solution.py:307
  42.1 0.0 copy-done
  42.1 0.1 copy.9
  42.2 0.1 reshape.16.refs_1_
  42.3 30.0 %all-to-all-done.1 = f32[256,8,128]{2,1,0:T(8,128)S(1)} async-done(((f32[256,8,128]{2,1,0:T(8,128)}), f32[256,8,128]{2,1,0:T(8,128)S(1)}, u32[]{:S(2)}, u32[]{:S(2)}) %all-to-all-start.1) | async-done | bytes 1048608 | tf_op jit(solution)/shard_map/all_to_all | solution.py:307
  72.3 3.9 %shift.1 = f32[64,32,8,128]{3,2,1,0:T(8,128)} custom-call(s32[8,128]{1,0:T(8,128)S(1)} %psum.7.refs_4_.refs_0_, s32[4,128]{1,0:T(4,128)S(1)} %reshape.16.refs_1_, f32[16,16,8,128]{3,2,1,0:T(8,128)S(1)} %bitcast.4, f32[8,2,8,128]{3,2,1,0:T(8,128)S(1)} %get-tuple-element.16.refs_3_), custom_call_target="tpu_custom_call" | custom-call | tf_op jit(solution)/shard_map/shift/pallas_call | solution.py:288
Async XLA Ops:
  0.0 42.1 %copy-start = (s32[64,8]{0,1:T(8,128)S(1)}, s32[64,8]{0,1:T(8,128)}, u32[]{:S(2)}) copy-start(s32[64,8]{0,1:T(8,128)} %param.9) | copy-start | bytes 6148
  2.7 24.2 %all-to-all-start = ((f32[16,16,8,128]{3,2,1,0:T(8,128)}), f32[16,16,8,128]{3,2,1,0:T(8,128)S(1)}, u32[]{:S(2)}, u32[]{:S(2)}) async-start(f32[16,16,8,128]{3,2,1,0:T(8,128)} %get-tuple-element.12), calls=%async_computation | async-start | bytes 2097152 | tf_op jit(solution)/shard_map/all_to_all | solution.py:304
  30.5 41.7 %all-to-all-start.1 = ((f32[256,8,128]{2,1,0:T(8,128)}), f32[256,8,128]{2,1,0:T(8,128)S(1)}, u32[]{:S(2)}, u32[]{:S(2)}) async-start(f32[256,8,128]{2,1,0:T(8,128)} %bitcast.1), calls=%async_computation.1 | async-start | bytes 2097152 | tf_op jit(solution)/shard_map/all_to_all | solution.py:307
